TPU v7x, 32 devices: a whole 2x2x4 slice. The times are simulated.
32 devices in a mesh: stream: 2 (over core), batch: 16 (over z, y, x).
Axes of the slice: x: 2, y: 2, z: 4, core: 2. Of those that a mesh axis runs over, the one named last changes fastest.
Arguments:
- tokens: bfloat16 [2, 16384, 768], P('stream', 'batch'), may hold values from -6 to 6
- lengths: int32 [2, 16, 8], P('stream', 'batch'), may hold values from 0 to 512, as said below
- attn_weight: float32 [4, 768, 768], P(None, 'batch', 'stream'), may hold values from -0.8660254 to 0.8660254
- attn_moment: float32 [4, 768, 768], P(None, 'batch', 'stream'), may hold values from -7168 to 7168
- attn_average: float32 [4, 768, 768], P(None, 'batch', 'stream'), may hold values from -0.21875 to 0.21875
- up_weight: float32 [768, 3072], P('batch', 'stream'), may hold values from -0.21875 to 0.21875
- up_moment: float32 [768, 3072], P('batch', 'stream'), may hold values from -3072 to 3072
- up_average: float32 [768, 3072], P('batch', 'stream'), may hold values from -0.21875 to 0.21875
- down_weight: float32 [3072, 768], P('batch', 'stream'), may hold values from -0.109375 to 0.109375
- down_moment: float32 [3072, 768], P('batch', 'stream'), may hold values from -4096 to 4096
- down_average: float32 [3072, 768], P('batch', 'stream'), may hold values from -0.109375 to 0.109375
- layer_vectors: float32 [8, 768], P('stream', 'batch'), may hold values from -0.4 to 1.4
- vector_moment: float32 [8, 768], P('stream', 'batch'), may hold values from -10240 to 10240
- vector_average: float32 [8, 768], P('stream', 'batch'), may hold values from -3 to 3
- up_bias: float32 [3072], P(('stream', 'batch')), may hold values from -0.625 to 0.625
- bias_moment: float32 [3072], P(('stream', 'batch')), may hold values from -4096 to 4096
- bias_average: float32 [3072], P(('stream', 'batch')), may hold values from -0.625 to 0.625
- pos_table: float32 [512, 768], P('stream', 'batch'), may hold values from -3 to 3
- pos_moment: float32 [512, 768], P('stream', 'batch'), may hold values from -5120 to 5120
- pos_average: float32 [512, 768], P('stream', 'batch'), may hold values from -3 to 3
Outputs:
- block_out: bfloat16 [2, 16384, 768], P('stream', 'batch')
- input_grad: float32 [2, 16384, 768], P('stream', 'batch')
- attn_grad: float32 [4, 768, 768], P(None, 'batch', 'stream')
- attn_moment_new: float32 [4, 768, 768], P(None, 'batch', 'stream')
- attn_weight_new: float32 [4, 768, 768], P(None, 'batch', 'stream')
- attn_average_new: float32 [4, 768, 768], P(None, 'batch', 'stream')
- up_grad: float32 [768, 3072], P('batch', 'stream')
- up_moment_new: float32 [768, 3072], P('batch', 'stream')
- up_weight_new: float32 [768, 3072], P('batch', 'stream')
- up_average_new: float32 [768, 3072], P('batch', 'stream')
- down_grad: float32 [3072, 768], P('batch', 'stream')
- down_moment_new: float32 [3072, 768], P('batch', 'stream')
- down_weight_new: float32 [3072, 768], P('batch', 'stream')
- down_average_new: float32 [3072, 768], P('batch', 'stream')
- vector_grad: float32 [8, 768], P('stream', 'batch')
- vector_moment_new: float32 [8, 768], P('stream', 'batch')
- vector_new: float32 [8, 768], P('stream', 'batch')
- vector_average_new: float32 [8, 768], P('stream', 'batch')
- bias_grad: float32 [3072], P(('stream', 'batch'))
- bias_moment_new: float32 [3072], P(('stream', 'batch'))
- bias_new: float32 [3072], P(('stream', 'batch'))
- bias_average_new: float32 [3072], P(('stream', 'batch'))
- pos_grad: float32 [512, 768], P('stream', 'batch')
- pos_moment_new: float32 [512, 768], P('stream', 'batch')
- pos_new: float32 [512, 768], P('stream', 'batch')
- pos_average_new: float32 [512, 768], P('stream', 'batch')
Inputs may be any that keep to these rules, and one draw needn't show every extreme that they name: `lengths`: for each pair index the two towers have the same number c of used slots, either 2 or 8; the used slots come first, the others are 0; a used slot's length lies between half of and all of 1024 // c, and one used slot of every device is full; in every draw some pair index has c = 2 and some has c = 8.
All inputs are finite; a program needn't handle non-finite values.
Results may differ from a plain program's by a relative error of at most 0.0075.
The roundings to bfloat16 on the way count: a program that leaves them out, or rounds other values in their place, can miss the bound.
Values may be sent and summed in bfloat16 or wider, within the bound.
No kernel may reach another device: no remote copies, remote signals or barrier semaphores. Data moves between devices by JAX's collectives and lax.ppermute only.
A program may use at most 192 MiB of HBM per device.

v0:
```python
import math

import jax
import jax.numpy as jnp
from jax import lax
from jax.sharding import PartitionSpec as P

HEADS = 12


EPS_NORM = 1e-06
INV_TEMP = 100.0
LOSS_WEIGHT = 256.0
MOMENTUM = 0.5
AVERAGE = 0.5
RATE = 0.0001
POS_RATE = 0.01
NEGATIVE = -1e30
ROOT_HALF = 0.7071067811865476
ROOT_TWO_PI = 2.5066282746310002


def swapped(block, axis, bit):
    count = lax.axis_size(axis)
    route = []
    for low in range(count):
        high = low | 1 << bit
        if high != low and high < count:
            route += [(low, high), (high, low)]
    return lax.ppermute(block, axis, route)


def halved(values):
    return values.astype(jnp.bfloat16)


def matmul(left, right):
    return jnp.dot(left, right, preferred_element_type=jnp.float32)


def gelu_value(values):
    return 0.5 * values * (1.0 + lax.erf(values * ROOT_HALF))


def gelu_slope(values):
    return (
        0.5 * (1.0 + lax.erf(values * ROOT_HALF))
        + values * jnp.exp(-0.5 * values * values) / ROOT_TWO_PI
    )


def layout(lengths_row, token_count):
    slot_count = lengths_row.shape[0]
    counted = jnp.sum((lengths_row > 0).astype(jnp.int32))
    bucket = token_count // counted
    places = jnp.arange(token_count, dtype=jnp.int32)
    document = places // bucket
    position = places - document * bucket
    member = document[:, None] == jnp.arange(slot_count, dtype=jnp.int32)[None, :]
    slot_length = jnp.sum(jnp.where(member, lengths_row[None, :], 0), axis=1)
    present = position < slot_length
    return (counted, position, present, member)


def norm_forward(values, gain_row, shift_row):
    center = values - jnp.mean(values, axis=-1, keepdims=True)
    inverse = lax.rsqrt(jnp.mean(center * center, axis=-1, keepdims=True) + EPS_NORM)
    normed = center * inverse
    return (normed * gain_row + shift_row, normed, inverse)


def norm_backward(grad_out, normed, inverse, gain_row):
    scaled = grad_out * gain_row
    inner = (
        scaled
        - jnp.mean(scaled, axis=-1, keepdims=True)
        - normed * jnp.mean(scaled * normed, axis=-1, keepdims=True)
    )
    return (inner * inverse, jnp.sum(grad_out * normed, axis=0), jnp.sum(grad_out, axis=0))


def slot_forward(query_half, key_half, value_half, present, slots, score_scale):
    token_count, heads, size = query_half.shape
    bucket = token_count // slots
    queries = query_half.reshape(slots, bucket, heads, size)
    keys = key_half.reshape(slots, bucket, heads, size)
    values = value_half.reshape(slots, bucket, heads, size)
    scores = (
        jnp.einsum("sqhd,skhd->shqk", queries, keys, preferred_element_type=jnp.float32)
        * score_scale
    )
    scores = jnp.where(present.reshape(slots, 1, 1, bucket), scores, NEGATIVE)
    highest = jnp.max(scores, axis=-1, keepdims=True)
    weights = jnp.exp(scores - highest)
    totals = jnp.sum(weights, axis=-1, keepdims=True)
    probs_half = halved(weights / totals)
    context = jnp.einsum(
        "shqk,skhd->sqhd", probs_half, values, preferred_element_type=jnp.float32
    ).reshape(token_count, heads, size)
    logsum = (
        (highest[..., 0] + jnp.log(totals[..., 0])).transpose(0, 2, 1).reshape(token_count, heads)
    )
    return (context, logsum)


def slot_backward(query_half, key_half, value_half, present, logsum, grad_half, slots, score_scale):
    token_count, heads, size = query_half.shape
    bucket = token_count // slots
    queries = query_half.reshape(slots, bucket, heads, size)
    keys = key_half.reshape(slots, bucket, heads, size)
    values = value_half.reshape(slots, bucket, heads, size)
    grads = grad_half.reshape(slots, bucket, heads, size)
    kept = logsum.reshape(slots, bucket, heads).transpose(0, 2, 1)[..., None]
    scores = (
        jnp.einsum("sqhd,skhd->shqk", queries, keys, preferred_element_type=jnp.float32)
        * score_scale
    )
    scores = jnp.where(present.reshape(slots, 1, 1, bucket), scores, NEGATIVE)
    probs = jnp.exp(scores - kept)
    dprob = jnp.einsum("sqhd,skhd->shqk", grads, values, preferred_element_type=jnp.float32)
    rowdot = jnp.sum(probs * dprob, axis=-1, keepdims=True)
    dscore = halved(probs * (dprob - rowdot))
    dquery = (
        jnp.einsum("shqk,skhd->sqhd", dscore, keys, preferred_element_type=jnp.float32)
        * score_scale
    )
    dkey = (
        jnp.einsum("shqk,sqhd->skhd", dscore, queries, preferred_element_type=jnp.float32)
        * score_scale
    )
    dvalue = jnp.einsum("shqk,sqhd->skhd", halved(probs), grads, preferred_element_type=jnp.float32)
    shape = (token_count, heads * size)
    return (dquery.reshape(shape), dkey.reshape(shape), dvalue.reshape(shape))


def renew(grad, moment, weight, average, rate):
    moment_new = MOMENTUM * moment + grad
    weight_new = weight - rate * (grad + MOMENTUM * moment_new)
    average_new = AVERAGE * average + (1.0 - AVERAGE) * weight_new
    return (grad, moment_new, weight_new, average_new)


def local(
    tokens,
    lengths,
    attn_weight,
    attn_moment,
    attn_average,
    up_weight,
    up_moment,
    up_average,
    down_weight,
    down_moment,
    down_average,
    layer_vectors,
    vector_moment,
    vector_average,
    up_bias,
    bias_moment,
    bias_average,
    pos_table,
    pos_moment,
    pos_average,
):
    sharded = (
        lax.all_gather(halved(attn_weight), "batch", axis=1, tiled=True),
        lax.all_gather(halved(up_weight), "batch", axis=0, tiled=True),
        lax.all_gather(halved(down_weight), "batch", axis=0, tiled=True),
        lax.all_gather(halved(layer_vectors), "batch", axis=1, tiled=True),
        lax.all_gather(halved(up_bias)[None, :], "batch", axis=1, tiled=True),
        lax.all_gather(halved(pos_table), "batch", axis=1, tiled=True),
    )
    gathered = (
        lax.all_gather(sharded[0], "stream", axis=2, tiled=True),
        lax.all_gather(sharded[1], "stream", axis=1, tiled=True),
        lax.all_gather(sharded[2], "stream", axis=1, tiled=True),
        lax.all_gather(sharded[3], "stream", axis=0, tiled=True),
        lax.all_gather(sharded[4], "stream", axis=0, tiled=True),
        lax.all_gather(sharded[5], "stream", axis=0, tiled=True),
    )
    attn_full, up_full, down_full, vector_half, bias_half, pos_full = gathered
    vectors = vector_half.astype(jnp.float32)
    bias_row = bias_half.reshape(-1).astype(jnp.float32)
    inputs = tokens[0].astype(jnp.float32)
    lengths_row = lengths[0, 0]
    token_count, width = inputs.shape
    slot_count = lengths_row.shape[0]
    head_size = width // HEADS
    score_scale = 1.0 / math.sqrt(head_size)
    counted, position, present, member = layout(lengths_row, token_count)
    hidden0 = inputs + jnp.take(pos_full, position, axis=0).astype(jnp.float32)
    entry = halved(hidden0)
    triple = jnp.einsum("td,pde->pte", entry, attn_full[:3], preferred_element_type=jnp.float32)
    query_half = halved(triple[0] + vectors[0]).reshape(token_count, HEADS, head_size)
    key_half = halved(triple[1]).reshape(token_count, HEADS, head_size)
    value_half = halved(triple[2] + vectors[1]).reshape(token_count, HEADS, head_size)
    context, logsum = lax.cond(
        counted == 2,
        lambda: slot_forward(query_half, key_half, value_half, present, 2, score_scale),
        lambda: slot_forward(query_half, key_half, value_half, present, slot_count, score_scale),
    )
    context_half = halved(context.reshape(token_count, width))
    resid1 = hidden0 + matmul(context_half, attn_full[3]) + vectors[2]
    hidden1, normed1, inverse1 = norm_forward(resid1, vectors[4], vectors[5])
    entry2 = halved(hidden1)
    pre_act = matmul(entry2, up_full) + bias_row
    active_half = halved(gelu_value(pre_act))
    resid2 = hidden1 + matmul(active_half, down_full) + vectors[3]
    hidden2, normed2, inverse2 = norm_forward(resid2, vectors[6], vectors[7])
    inverse_len = 1.0 / jnp.maximum(lengths_row, 1).astype(jnp.float32)
    pool = jnp.where(member & present[:, None], inverse_len[None, :], 0.0)
    pooled = jnp.dot(pool.T, hidden2, precision=lax.Precision.HIGHEST)
    inverse_norm = lax.rsqrt(jnp.sum(pooled * pooled, axis=-1, keepdims=True) + EPS_NORM)
    unit_half = halved(pooled * inverse_norm)
    row_live = (lengths_row > 0).astype(jnp.float32)
    live_half = halved(row_live)
    batch_index = lax.axis_index("batch")
    pair_total = lax.axis_size("batch") * slot_count
    partner = swapped(unit_half, "stream", 0)
    others, other_live = (
        lax.all_gather(partner, "batch", axis=0, tiled=True),
        lax.all_gather(live_half, "batch", axis=0, tiled=True),
    )
    logits = (
        jnp.einsum("sd,md->sm", unit_half, others, preferred_element_type=jnp.float32) * INV_TEMP
    )
    logits = jnp.where(other_live[None, :] > 0, logits, NEGATIVE)
    highest = jnp.max(logits, axis=-1, keepdims=True)
    weights = jnp.exp(logits - highest)
    probs = weights / jnp.sum(weights, axis=-1, keepdims=True)
    own_rows = batch_index * slot_count + jnp.arange(slot_count, dtype=jnp.int32)
    target = (jnp.arange(pair_total, dtype=jnp.int32)[None, :] == own_rows[:, None]).astype(
        jnp.float32
    )
    dlogit_half = halved(LOSS_WEIGHT * (probs - target) * row_live[:, None])
    own_grad = (
        jnp.einsum("sm,md->sd", dlogit_half, others, preferred_element_type=jnp.float32) * INV_TEMP
    )
    other_grad = (
        jnp.einsum("sm,sd->md", dlogit_half, unit_half, preferred_element_type=jnp.float32)
        * INV_TEMP
    )
    summed = lax.psum_scatter(other_grad, "batch", scatter_dimension=0, tiled=True)
    returned = swapped(summed, "stream", 0)
    dunit = own_grad + returned
    along = jnp.sum(pooled * dunit, axis=-1, keepdims=True)
    dpooled = inverse_norm * dunit - inverse_norm * inverse_norm * inverse_norm * pooled * along
    dhidden2 = jnp.dot(pool, dpooled, precision=lax.Precision.HIGHEST)
    dresid2, dgain2, dshift2 = norm_backward(dhidden2, normed2, inverse2, vectors[6])
    dresid2_half = halved(dresid2)
    down_grad = jnp.einsum(
        "tf,td->fd", active_half, dresid2_half, preferred_element_type=jnp.float32
    )
    dactive = jnp.einsum("td,fd->tf", dresid2_half, down_full, preferred_element_type=jnp.float32)
    dpre = dactive * gelu_slope(pre_act)
    dpre_half = halved(dpre)
    up_grad = jnp.einsum("td,tf->df", entry2, dpre_half, preferred_element_type=jnp.float32)
    dhidden1 = dresid2 + jnp.einsum(
        "tf,df->td", dpre_half, up_full, preferred_element_type=jnp.float32
    )
    dresid1, dgain1, dshift1 = norm_backward(dhidden1, normed1, inverse1, vectors[4])
    dresid1_half = halved(dresid1)
    out_grad = jnp.einsum(
        "td,te->de", context_half, dresid1_half, preferred_element_type=jnp.float32
    )
    dcontext_half = halved(
        jnp.einsum("te,de->td", dresid1_half, attn_full[3], preferred_element_type=jnp.float32)
    ).reshape(token_count, HEADS, head_size)
    dquery, dkey, dvalue = lax.cond(
        counted == 2,
        lambda: slot_backward(
            query_half, key_half, value_half, present, logsum, dcontext_half, 2, score_scale
        ),
        lambda: slot_backward(
            query_half,
            key_half,
            value_half,
            present,
            logsum,
            dcontext_half,
            slot_count,
            score_scale,
        ),
    )
    dtriple_half = halved(jnp.stack([dquery, dkey, dvalue]))
    in_grads = jnp.einsum("td,pte->pde", entry, dtriple_half, preferred_element_type=jnp.float32)
    dhidden0 = dresid1 + jnp.einsum(
        "pte,pde->td", dtriple_half, attn_full[:3], preferred_element_type=jnp.float32
    )
    long_rows = token_count // 2
    short_rows = token_count // slot_count
    long_sum = jnp.sum(dhidden0.reshape(2, long_rows, width), axis=0)
    short_sum = jnp.sum(dhidden0.reshape(slot_count, short_rows, width), axis=0)
    short_full = jnp.concatenate(
        [short_sum, jnp.zeros((long_rows - short_rows, width), jnp.float32)], axis=0
    )
    pos_row_grad = jnp.where(counted == 2, long_sum, short_full)
    attn_term = jnp.concatenate([in_grads, out_grad[None]], axis=0)
    vector_term = jnp.stack(
        [
            jnp.sum(dquery, axis=0),
            jnp.sum(dvalue, axis=0),
            jnp.sum(dresid1, axis=0),
            jnp.sum(dresid2, axis=0),
            dgain1,
            dshift1,
            dgain2,
            dshift2,
        ]
    )
    bias_term = jnp.sum(dpre, axis=0).reshape(lax.axis_size("stream"), -1)
    partial_value = (
        lax.psum_scatter(attn_term, "batch", scatter_dimension=1, tiled=True),
        lax.psum_scatter(up_grad, "batch", scatter_dimension=0, tiled=True),
        lax.psum_scatter(down_grad, "batch", scatter_dimension=0, tiled=True),
        lax.psum_scatter(vector_term, "batch", scatter_dimension=1, tiled=True),
        lax.psum_scatter(bias_term, "batch", scatter_dimension=1, tiled=True),
        lax.psum_scatter(pos_row_grad, "batch", scatter_dimension=1, tiled=True),
    )
    reduced = (
        lax.psum_scatter(partial_value[0], "stream", scatter_dimension=2, tiled=True),
        lax.psum_scatter(partial_value[1], "stream", scatter_dimension=1, tiled=True),
        lax.psum_scatter(partial_value[2], "stream", scatter_dimension=1, tiled=True),
        lax.psum_scatter(partial_value[3], "stream", scatter_dimension=0, tiled=True),
        lax.psum_scatter(partial_value[4], "stream", scatter_dimension=0, tiled=True),
        lax.psum_scatter(partial_value[5], "stream", scatter_dimension=0, tiled=True),
    )
    attn_all = renew(reduced[0], attn_moment, attn_weight, attn_average, RATE)
    up_all = renew(reduced[1], up_moment, up_weight, up_average, RATE)
    down_all = renew(reduced[2], down_moment, down_weight, down_average, RATE)
    vector_all = renew(reduced[3], vector_moment, layer_vectors, vector_average, RATE)
    bias_all = renew(reduced[4].reshape(-1), bias_moment, up_bias, bias_average, RATE)
    pos_all = renew(reduced[5], pos_moment, pos_table, pos_average, POS_RATE)
    return (
        halved(hidden2)[None],
        dhidden0[None],
        attn_all[0],
        attn_all[1],
        attn_all[2],
        attn_all[3],
        up_all[0],
        up_all[1],
        up_all[2],
        up_all[3],
        down_all[0],
        down_all[1],
        down_all[2],
        down_all[3],
        vector_all[0],
        vector_all[1],
        vector_all[2],
        vector_all[3],
        bias_all[0],
        bias_all[1],
        bias_all[2],
        bias_all[3],
        pos_all[0],
        pos_all[1],
        pos_all[2],
        pos_all[3],
    )


def solution(mesh):
    in_specs = (
        P("stream", "batch", None),
        P("stream", "batch", None),
        P(None, "batch", "stream"),
        P(None, "batch", "stream"),
        P(None, "batch", "stream"),
        P("batch", "stream"),
        P("batch", "stream"),
        P("batch", "stream"),
        P("batch", "stream"),
        P("batch", "stream"),
        P("batch", "stream"),
        P("stream", "batch"),
        P("stream", "batch"),
        P("stream", "batch"),
        P(("stream", "batch")),
        P(("stream", "batch")),
        P(("stream", "batch")),
        P("stream", "batch"),
        P("stream", "batch"),
        P("stream", "batch"),
    )
    out_specs = (
        P("stream", "batch", None),
        P("stream", "batch", None),
        P(None, "batch", "stream"),
        P(None, "batch", "stream"),
        P(None, "batch", "stream"),
        P(None, "batch", "stream"),
        P("batch", "stream"),
        P("batch", "stream"),
        P("batch", "stream"),
        P("batch", "stream"),
        P("batch", "stream"),
        P("batch", "stream"),
        P("batch", "stream"),
        P("batch", "stream"),
        P("stream", "batch"),
        P("stream", "batch"),
        P("stream", "batch"),
        P("stream", "batch"),
        P(("stream", "batch")),
        P(("stream", "batch")),
        P(("stream", "batch")),
        P(("stream", "batch")),
        P("stream", "batch"),
        P("stream", "batch"),
        P("stream", "batch"),
        P("stream", "batch"),
    )
    return jax.shard_map(local, mesh=mesh, in_specs=in_specs, out_specs=out_specs, check_vma=False)
```

profile of v0, /device:TPU:0, one launch (start us, length us, event | category | flops | bytes accessed | tf_op | source)
XLA Modules:
  0.0 1802.5 jit_solution(18286727534438900666)
XLA Ops:
  12.4 64.0 %all-gather.12.cloned.1.call-done = bf16[4,768,384]{2,1,0:T(8,128)(2,1)} async-done(((bf16[4,48,384]{2,1,0:T(8,128)(2,1)}), bf16[4,768,384]{2,1,0:T(8,128)(2,1)}) %all-gather.12.cloned.1.call-update) | async-done | bytes 2359312 | tf_op jit(solution)/shard_map/all_gather | solution.py:166
  76.5 64.4 %all-gather.16.cloned.1.call-done = bf16[768,1536]{1,0:T(8,128)(2,1)} async-done(((bf16[48,1536]{1,0:T(8,128)(2,1)}), bf16[768,1536]{1,0:T(8,128)(2,1)}) %all-gather.16.cloned.1.call-update) | async-done | bytes 2359312 | tf_op jit(solution)/shard_map/all_gather | solution.py:167
  145.5 42.0 %all_gather.42 = bf16[256,768]{0,1:T(8,128)(2,1)S(1)} all-gather(bf16[256,48]{0,1:T(8,128)(2,1)S(1)} %convert_element_type.140), channel_id=1, replica_groups=mesh['stream'=2,'batch'=16] {'batch'}, dimensions={1}, use_global_device_ids=true | all-gather | bytes 417792 | tf_op jit(solution)/shard_map/all_gather | solution.py:171
  188.2 37.6 %all-reduce.7 = (bf16[1536]{0:T(1024)(128)(2,1)S(1)}, bf16[128]{0:T(256)(128)(2,1)S(1)}) all-reduce(bf16[1536]{0:T(1024)(128)(2,1)S(1)} %dynamic-update-slice, bf16[128]{0:T(256)(128)(2,1)S(1)} %dynamic-update-slice.1), channel_id=2, replica_groups=mesh['stream'=2,'batch'=16] {'batch'}, use_global_device_ids=true, to_apply=%add.1 | all-reduce | flops 1664 | bytes 6656
  231.6 37.1 %all-gather.2 = bf16[16,48,4]{1,2,0:T(4,128)(2,1)S(1)} all-gather(bf16[1,48,4]{1,2,0:T(4,128)(2,1)S(1)} %convert_bitcast_fusion), channel_id=1, replica_groups=mesh['stream'=2,'batch'=16] {'batch'}, dimensions={0}, use_global_device_ids=true | all-gather | bytes 6528 | tf_op jit(solution)/shard_map/all_gather | solution.py:169
  270.6 4.0 gather_fusion
  275.8 6.6 convolution_bitcast_fusion
  284.3 65.7 %conditional.2 = (f32[1024,12]{1,0:T(8,128)}, bf16[1024,768]{0,1:T(8,128)(2,1)}) conditional(s32[]{:T(128)} %convert_element_type.142, (pred[1024]{0:T(1024)(128)(4,1)S(1)}, bf16[1024,768]{1,0:T(8,128)(2,1)}, bf16[1024,768]{1,0:T(8,128)(2,1)S(1)}, bf16[1024,768]{1,0:T(8,128)(2,1)S(1)}) %tuple.34, (pred[1024]{0:T(1024)(128)(4,1)S(1)}, ...), branch_computations={%region_2.5_spmd, %region_5.8_spmd} | conditional | flops 1686884352 | bytes 113742888 | solution.py:197
  294.0 3.9 reshape_reshape.41
  299.5 3.8 reshape_reshape.40
  303.4 2.6 copy.439
  306.0 3.8 reshape_reshape.39
  309.8 13.0 fusion.14
  322.8 11.2 fusion.15
  334.1 11.4 fusion.22
  350.1 4.7 fusion.141
  357.0 12.3 multiply_convert_fusion.4
  369.3 9.3 fusion.142
  382.7 36.8 %all_gather.55 = bf16[128,768]{1,0:T(8,128)(2,1)S(1)} all-gather(bf16[8,768]{1,0:T(8,128)(2,1)S(1)} %collective-permute-done), channel_id=1, replica_groups=mesh['stream'=2,'batch'=16] {'batch'}, dimensions={0}, use_global_device_ids=true | all-gather | bytes 208896 | tf_op jit(solution)/shard_map/all_gather | solution.py:221
  421.2 118.9 %reduce-scatter.19.cloned.1.call-done = f32[8,768]{1,0:T(8,128)} async-done(((f32[128,768]{1,0:T(8,128)}), f32[8,768]{1,0:T(8,128)}) %reduce-scatter.19.cloned.1.call-update) | async-done | bytes 24592 | tf_op jit(solution)/shard_map/reduce_scatter | solution.py:243
  541.8 6.6 multiply_reduce_fusion.2
  548.4 3.6 fusion.138
  552.0 13.6 fusion.144
  565.7 6.5 multiply_reduce_fusion.3
  574.1 4.7 convolution_convert_fusion
  578.8 134.5 %conditional.3 = (f32[1,768]{1,0:T(1,128)S(1)}, f32[1,768]{1,0:T(1,128)S(1)}, bf16[1,1024,768]{2,1,0:T(8,128)(2,1)S(1)}, bf16[1,1024,768]{2,1,0:T(8,128)(2,1)}, bf16[1,1024,768]{2,1,0:T(8,128)(2,1)}) conditional(s32[]{:T(128)} %convert_element_type.142, (pred[1024]{0:T(1024)(128)(4,1)S(1)}, bf16[1024,768]{1,0:T(8,128)(2,1)}, ...), branch_computations={%region_21.25_spmd, %region_25.29_spmd} | conditional | flops 4127181312 | bytes 296066208 | solution.py:269
  588.0 4.0 reshape_reshape.49
  594.8 3.9 reshape_reshape.48
  600.3 2.9 reshape_reshape.47
  604.8 2.9 reshape_reshape.46
  607.7 10.1 fusion.58
  617.8 12.6 bitcast_reduce_fusion.2
  630.5 3.0 copy.433
  635.8 2.7 copy.493
  638.5 21.5 %multiply_reduce_fusion.1 = (f32[2,12,512]{2,1,0:T(8,128)S(1)}, f32[2,12,512,512]{2,3,1,0:T(8,128)}) fusion(f32[2,12,512,512]{2,3,1,0:T(8,128)} %fusion.58, f32[2,12,512]{2,1,0:T(8,128)S(1)} %bitcast.243, pred[2,512]{1,0:T(4,128)(4,1)S(1)} %broadcast_in_dim.127, bf16[2,512,12,64]{1,0,3,2:T(2,128)(2,1)S(1)} %copy-done.19, ...), kind=kOutput, calls=%fused_computation.61 | convolution fusion | flops 836751360 | bytes 53576704 | tf_op jit(solution)/shard_map/cond/branch_1_fun/sqhd,skhd->shqk/dot_general | solution.py:120
  660.1 21.5 %multiply_convert_fusion.2 = bf16[2,12,512,512]{2,3,1,0:T(8,128)(2,1)} fusion(f32[2,12,512,512]{2,3,1,0:T(8,128)} %get-tuple-element.456, f32[2,12,512,512]{2,3,1,0:T(8,128)} %fusion.58, f32[2,12,512]{2,1,0:T(8,128)S(1)} %get-tuple-element.455, f32[2,12,512]{2,1,0:T(8,128)S(1)} %bitcast.244, pred[2,512]{1,0:T(4,128)(4,1)S(1)} %broadcast_in_dim.127), kind=kLoop, calls=%fused_computation.60 | loop fusion | flops 37748736 | bytes 63013888 | tf_op jit(solution)/shard_map/cond/branch_1_fun/convert_element_type | solution.py:34
  681.6 9.6 fusion.53
  691.2 7.3 bitcast_reduce_fusion.3
  698.6 4.2 copy.432
  702.8 3.8 reshape.295
  706.6 2.6 copy.491
  716.7 7.6 bitcast_add_fusion
  726.5 2.7 pad_select_fusion
  729.1 3.2 copy.486
  732.4 3.0 convolution_bitcast_fusion.2
  735.5 6.5 convolution_bitcast_fusion.1
  742.0 4.3 pad_maximum_fusion
  746.2 12.1 copy.457
  760.2 10.8 fusion.73
  774.4 10.2 fusion.100
  784.7 71.5 %reduce-scatter.37.cloned.1.call-done = f32[48,512]{1,0:T(8,128)} async-done(((f32[768,512]{1,0:T(8,128)}), f32[48,512]{1,0:T(8,128)}) %reduce-scatter.37.cloned.1.call-update) | async-done | bytes 98320
  856.9 286.0 %all-reduce.10.cloned.1.call-done = f32[4,768,768]{2,0,1:T(4,128)} async-done(((f32[4,768,768]{2,0,1:T(4,128)}), f32[4,768,768]{2,0,1:T(4,128)}) %all-reduce.10.cloned.1.call-update) | async-done | bytes 9437200
  1144.0 12.3 copy.480
  1156.3 13.4 reshape.333
  1169.8 149.5 %reduce-scatter.21.cloned.1.call-done = f32[48,3072]{1,0:T(8,128)} async-done(((f32[768,3072]{1,0:T(8,128)}), f32[48,3072]{1,0:T(8,128)}) %reduce-scatter.21.cloned.1.call-update) | async-done | bytes 589840 | tf_op jit(solution)/shard_map/reduce_scatter | solution.py:314
  1320.6 124.7 %reduce-scatter.35.cloned.1.call-done = f32[96,2]{1,0:T(8,128)} async-done(((f32[1536,2]{1,0:T(8,128)}), f32[96,2]{1,0:T(8,128)}) %reduce-scatter.35.cloned.1.call-update) | async-done | bytes 784
  1446.2 124.4 %reduce-scatter.33.cloned.1.call-done = f32[48,8]{1,0:T(8,128)} async-done(((f32[768,8]{1,0:T(8,128)}), f32[48,8]{1,0:T(8,128)}) %reduce-scatter.33.cloned.1.call-update) | async-done | bytes 1552
  1571.4 2.5 all-reduce.6
  1574.5 173.0 %reduce-scatter.25.cloned.1.call-done = f32[192,768]{1,0:T(8,128)} async-done(((f32[3072,768]{1,0:T(8,128)}), f32[192,768]{1,0:T(8,128)}) %reduce-scatter.25.cloned.1.call-update) | async-done | bytes 589840 | tf_op jit(solution)/shard_map/reduce_scatter | solution.py:315
  1748.8 7.9 reduce-scatter.29.cloned.1.call-done
  1758.1 10.0 reduce-scatter.31.cloned.1.call-done
  1768.2 7.3 reshape.334
  1775.5 7.2 copy.462
  1782.7 6.5 copy.481
  (278 shorter events, 74.5 us)
Async XLA Ops:
  7.2 69.2 %all-gather.12.cloned.1.call-start = ((), (), s32[]{:S(2)}) async-start(), calls=%async_computation.10 | async-start | bytes 2506752 | tf_op jit(solution)/shard_map/all_gather | solution.py:166
  8.9 132.1 %copy-start.68 = (s32[1,1,8]{2,1,0:T(1,128)S(1)}, s32[1,1,8]{2,1,0:T(1,128)}, u32[]{:S(2)}) copy-start(s32[1,1,8]{2,1,0:T(1,128)} %param.25) | copy-start | bytes 100
  8.9 134.7 %copy-start.65 = (u32[32]{0:T(128)S(1)}, u32[32]{0:T(128)}, u32[]{:S(2)}) copy-start(u32[32]{0:T(128)} %constant.139) | copy-start | bytes 388
  8.9 136.6 %copy-start.69 = (f32[96]{0:T(128)S(1)}, f32[96]{0:T(128)}, u32[]{:S(2)}) copy-start(f32[96]{0:T(128)} %param.38) | copy-start | bytes 1156
  8.9 136.6 %copy-start.46 = (f32[256,48]{0,1:T(8,128)S(1)}, f32[256,48]{0,1:T(8,128)}, u32[]{:S(2)}) copy-start(f32[256,48]{0,1:T(8,128)} %param.41) | copy-start | bytes 147460
  8.9 132.0 %all-gather.16.cloned.1.call-start = ((), (), s32[]{:S(2)}) async-start(), calls=%async_computation.12 | async-start | bytes 2506752 | tf_op jit(solution)/shard_map/all_gather | solution.py:167
  10.6 218.2 %all-gather.20.cloned.1.call-start = ((), (), s32[]{:S(2)}) async-start(), calls=%async_computation.14 | async-start | bytes 2506752 | tf_op jit(solution)/shard_map/all_gather | solution.py:168
  12.4 262.5 %all-gather.14.cloned.1.call-start = ((), (), s32[]{:S(2)}) async-start(), calls=%async_computation.11 | async-start | bytes 7077888 | tf_op jit(solution)/shard_map/all_gather | solution.py:174
  76.4 152.4 %copy-start.57 = (f32[4,48]{1,0:T(4,128)S(1)}, f32[4,48]{1,0:T(4,128)}, u32[]{:S(2)}) copy-start(f32[4,48]{1,0:T(4,128)} %param.35) | copy-start | bytes 2308
  76.4 280.6 %all-gather.18.cloned.1.call-start = ((), (), s32[]{:S(2)}) async-start(), calls=%async_computation.13 | async-start | bytes 7077888 | tf_op jit(solution)/shard_map/all_gather | solution.py:175
  140.9 228.4 %all-gather.22.cloned.1.call-start = ((), (), s32[]{:S(2)}) async-start(), calls=%async_computation.15 | async-start | bytes 7077888 | tf_op jit(solution)/shard_map/all_gather | solution.py:176
  228.9 311.2 %reduce-scatter.19.cloned.1.call-start = ((), (), s32[]{:S(2)}) async-start(), calls=%async_computation.16 | async-start | bytes 417792 | tf_op jit(solution)/shard_map/reduce_scatter | solution.py:243
  229.0 121.0 %copy-start.66 = (pred[1024]{0:T(1024)(128)(4,1)}, pred[1024]{0:T(1024)(128)(4,1)S(1)}, u32[]{:S(2)}) copy-start(pred[1024]{0:T(1024)(128)(4,1)S(1)} %compare_and_fusion) | copy-start | bytes 3076
  274.7 94.6 %copy-start.50 = (f32[768]{0:T(1024)}, f32[768]{0:T(1024)S(1)}, u32[]{:S(2)}) copy-start(f32[768]{0:T(1024)S(1)} %get-tuple-element.413) | copy-start | bytes 9220
  274.7 297.5 %copy-start.48 = (f32[768]{0:T(1024)}, f32[768]{0:T(1024)S(1)}, u32[]{:S(2)}) copy-start(f32[768]{0:T(1024)S(1)} %get-tuple-element.414) | copy-start | bytes 9220
  322.8 11.2 copy-start.27
  354.8 217.5 %copy-start.36 = (f32[1024]{0:T(1024)}, f32[1024]{0:T(1024)S(1)}, u32[]{:S(2)}) copy-start(f32[1024]{0:T(1024)S(1)} %broadcast_multiply_fusion.5) | copy-start | bytes 12292
  357.0 215.2 %copy-start.44 = (f32[1024]{0:T(1024)}, f32[1024]{0:T(1024)S(1)}, u32[]{:S(2)}) copy-start(f32[1024]{0:T(1024)S(1)} %add_rsqrt_fusion.1) | copy-start | bytes 12292
  378.7 2.8 copy-start.6
  381.5 1.2 collective-permute-start
  421.1 435.0 %reduce-scatter.37.cloned.1.call-start = ((), (), s32[]{:S(2)}) async-start(), calls=%async_computation.25 | async-start | bytes 1671168
  540.1 1.4 collective-permute-start.1
  541.8 6.6 copy-start.7
  548.4 17.3 slice-start.2
  552.0 13.7 copy-start.22
  552.0 13.7 copy-start.4
  552.0 13.7 slice-start.3
  565.7 6.6 copy-start.14
  574.1 4.7 copy-start.24
  588.0 5.2 copy-start.16
  598.7 4.5 copy-start.2
  603.2 4.5 copy-start.10
  607.7 10.1 copy-start.21
  716.7 7.6 copy-start.35
  729.1 3.3 copy-start.26
  732.3 3.1 copy-start.67
  732.4 410.5 %all-reduce.10.cloned.1.call-start = ((), (), s32[]{:S(2)}) async-start(), calls=%async_computation.26 | async-start | bytes 18874368
  732.4 3.1 copy-start.31
  732.4 3.1 copy-start.73
  758.4 560.9 %reduce-scatter.21.cloned.1.call-start = ((), (), s32[]{:S(2)}) async-start(), calls=%async_computation.17 | async-start | bytes 10027008 | tf_op jit(solution)/shard_map/reduce_scatter | solution.py:314
  771.1 3.3 copy-start.23
  771.1 674.3 %reduce-scatter.35.cloned.1.call-start = ((), (), s32[]{:S(2)}) async-start(), calls=%async_computation.24 | async-start | bytes 835584
  773.0 797.7 %reduce-scatter.33.cloned.1.call-start = ((), (), s32[]{:S(2)}) async-start(), calls=%async_computation.23 | async-start | bytes 417792
  774.1 973.4 %reduce-scatter.25.cloned.1.call-start = ((), (), s32[]{:S(2)}) async-start(), calls=%async_computation.19 | async-start | bytes 10027008 | tf_op jit(solution)/shard_map/reduce_scatter | solution.py:315
  784.7 972.0 %reduce-scatter.29.cloned.1.call-start = ((), (), s32[]{:S(2)}) async-start(), calls=%async_computation.21 | async-start | bytes 147456 | tf_op jit(solution)/shard_map/reduce_scatter | solution.py:326
  856.2 912.0 %reduce-scatter.31.cloned.1.call-start = ((), (), s32[]{:S(2)}) async-start(), calls=%async_computation.22 | async-start | bytes 1179648
  1156.2 163.2 %copy-start.74 = (u32[32]{0:T(128)S(1)}, u32[32]{0:T(128)}, u32[]{:S(2)}) copy-start(u32[32]{0:T(128)} %constant.155) | copy-start | bytes 388
  1156.2 417.7 %copy-start.58 = (f32[4,48]{1,0:T(4,128)S(1)}, f32[4,48]{1,0:T(4,128)}, u32[]{:S(2)}) copy-start(f32[4,48]{1,0:T(4,128)} %param.35) | copy-start | bytes 2308
  1156.2 417.7 %copy-start.63 = (f32[4,48]{1,0:T(4,128)S(1)}, f32[4,48]{1,0:T(4,128)}, u32[]{:S(2)}) copy-start(f32[4,48]{1,0:T(4,128)} %param.37) | copy-start | bytes 2308
  1156.2 417.7 %copy-start.64 = (f32[4,48]{1,0:T(4,128)S(1)}, f32[4,48]{1,0:T(4,128)}, u32[]{:S(2)}) copy-start(f32[4,48]{1,0:T(4,128)} %param.36) | copy-start | bytes 2308
  1156.2 591.3 %copy-start.70 = (f32[96]{0:T(128)S(1)}, f32[96]{0:T(128)}, u32[]{:S(2)}) copy-start(f32[96]{0:T(128)} %param.38) | copy-start | bytes 1156
  1156.2 591.3 %copy-start.71 = (f32[96]{0:T(128)S(1)}, f32[96]{0:T(128)}, u32[]{:S(2)}) copy-start(f32[96]{0:T(128)} %param.40) | copy-start | bytes 1156
  1156.2 591.3 %copy-start.72 = (f32[96]{0:T(128)S(1)}, f32[96]{0:T(128)}, u32[]{:S(2)}) copy-start(f32[96]{0:T(128)} %param.39) | copy-start | bytes 1156
  1156.3 600.4 %copy-start.47 = (f32[256,48]{0,1:T(8,128)S(1)}, f32[256,48]{0,1:T(8,128)}, u32[]{:S(2)}) copy-start(f32[256,48]{0,1:T(8,128)} %param.41) | copy-start | bytes 147460
  1156.3 600.4 %copy-start.52 = (f32[256,48]{0,1:T(8,128)S(1)}, f32[256,48]{0,1:T(8,128)}, u32[]{:S(2)}) copy-start(f32[256,48]{0,1:T(8,128)} %param.43) | copy-start | bytes 147460
  1156.3 600.4 %copy-start.53 = (f32[256,48]{0,1:T(8,128)S(1)}, f32[256,48]{0,1:T(8,128)}, u32[]{:S(2)}) copy-start(f32[256,48]{0,1:T(8,128)} %param.42) | copy-start | bytes 147460
  1169.8 622.1 %reduce-scatter.23.cloned.1.call-start = ((), (), s32[]{:S(2)}) async-start(), calls=%async_computation.18 | async-start | bytes 884736 | tf_op jit(solution)/shard_map/reduce_scatter | solution.py:322
  1319.3 474.5 %reduce-scatter.27.cloned.1.call-start = ((), (), s32[]{:S(2)}) async-start(), calls=%async_computation.20 | async-start | bytes 884736 | tf_op jit(solution)/shard_map/reduce_scatter | solution.py:323
  1782.7 6.5 copy-start.32
  1782.7 6.5 copy-start.38
  1782.7 6.5 copy-start.39
  1789.2 4.6 copy-start.34
  1789.2 4.6 copy-start.42
  1789.2 4.6 copy-start.43
  (22 other events, 43.5 us)
Sparse Core Ops, SparseCore 0:
  11.3 65.0 all-gather.11
  79.8 61.0 all-gather.15
  144.3 62.7 all-gather.19
  208.4 13.3 all-gather.13
  223.2 15.6 all-gather.17
  240.3 15.4 all-gather.21
  421.3 118.7 reduce-scatter.18
  732.5 123.6 reduce-scatter.36
  863.3 279.4 all-reduce.9
  1149.3 169.9 reduce-scatter.20
  1324.0 121.2 reduce-scatter.34
  1449.9 120.6 reduce-scatter.32
  1577.2 170.2 reduce-scatter.24
  1750.2 6.4 reduce-scatter.28
  1758.8 9.3 reduce-scatter.30
  1771.0 9.1 reduce-scatter.22
  1782.9 9.1 reduce-scatter.26
where the time goes:
time: 1810 us; the launch traced here: 1800 us
  waiting for transfers between devices  1200 us (66%)
  matrix products  192 us (11%)
  blocking collectives  162 us (9%)
  local copies, waits for them, and re-layouts  149 us (8%)
  other arithmetic  64.8 us (4%)
  between operations  20.4 us (1%)
    unnamed x22, waiting for transfers between devices  617 us
    reduce_scatter x1, waiting for transfers between devices, local(): lax.psum_scatter(down_grad, 'batch', scatter_dimension=0, tiled=True)  173 us
    reduce_scatter x1, waiting for transfers between devices, local(): lax.psum_scatter(up_grad, 'batch', scatter_dimension=0, tiled=True)  150 us
    reduce_scatter x1, waiting for transfers between devices, local(): lax.psum_scatter(other_grad, 'batch', scatter_dimension=0, tiled=True)  119 us
    unnamed x146, local copies, waits for them, and re-layouts  67.2 us
    all_gather x1, waiting for transfers between devices, local(): lax.all_gather(halved(up_weight), 'batch', axis=0, tiled=True)  64.4 us
    all_gather x1, waiting for transfers between devices, local(): lax.all_gather(halved(attn_weight), 'batch', axis=1, tiled=True)  64 us
    all_gather x1, blocking collectives, local(): lax.all_gather(halved(pos_table), 'batch', axis=1, tiled=True)  42 us
  transfers between devices with their start and end apart: 19, of which 13 were waited for; matrix products, arithmetic and copies ran while one was open for 11% of the time, Pallas kernels for 0%

commit v1 on v0

--- a/solution.py
+++ b/solution.py
@@ -20,14 +20,97 @@
 ROOT_TWO_PI = 2.5066282746310002
 
 
-def swapped(block, axis, bit):
+def exchanged(block, axis, bit):
     count = lax.axis_size(axis)
-    route = []
-    for low in range(count):
-        high = low | 1 << bit
-        if high != low and high < count:
-            route += [(low, high), (high, low)]
+    route = [(place, place ^ (1 << bit)) for place in range(count)]
     return lax.ppermute(block, axis, route)
+
+
+def bit_at(axis, bit):
+    return (lax.axis_index(axis) >> bit) & 1
+
+
+def batch_bits():
+    return lax.axis_size("batch").bit_length() - 1
+
+
+def joined(mine, other, upper, dim):
+    low = jnp.where(upper, other, mine)
+    high = jnp.where(upper, mine, other)
+    return jnp.stack([low, high], axis=dim)
+
+
+def gather_pair(block):
+    bits = batch_bits()
+    for depth, bit in enumerate(range(bits - 1, 1, -1)):
+        other = exchanged(block, "batch", bit)
+        block = joined(block, other, bit_at("batch", bit) == 1, depth)
+    halves = []
+    depth = bits - 2
+    first = jnp.take(block, 0, axis=depth)
+    second = jnp.take(block, 1, axis=depth)
+    first_other = exchanged(first, "batch", 1)
+    second_other = exchanged(second, "batch", 0)
+    first = joined(first, first_other, bit_at("batch", 1) == 1, depth)
+    second = joined(second, second_other, bit_at("batch", 0) == 1, depth)
+    first_other = exchanged(first, "batch", 0)
+    second_other = exchanged(second, "batch", 1)
+    first = joined(first, first_other, bit_at("batch", 0) == 1, depth + 1)
+    second = joined(second, second_other, bit_at("batch", 1) == 1, depth)
+    shape = (-1, block.shape[-1])
+    return first.reshape(shape), second.reshape(shape)
+
+
+def packed(values, wide):
+    if not wide:
+        return halved(values)
+    plain, kept = values[..., :-wide], values[..., -wide:]
+    coarse = lax.reduce_precision(kept, exponent_bits=8, mantissa_bits=7)
+    return halved(jnp.concatenate([plain, coarse, kept - coarse], axis=-1))
+
+
+def unpacked(block, wide):
+    values = block.astype(jnp.float32)
+    if not wide:
+        return values
+    plain, coarse, rest = values[..., : -2 * wide], values[..., -2 * wide : -wide], values[..., -wide:]
+    return jnp.concatenate([plain, coarse + rest], axis=-1)
+
+
+def fold(block, axis, bit, dim, wide=0):
+    upper = bit_at(axis, bit)
+    sent = packed(lax.dynamic_index_in_dim(block, 1 - upper, dim, keepdims=False), wide)
+    kept = lax.dynamic_index_in_dim(block, upper, dim, keepdims=False)
+    return kept + unpacked(exchanged(sent, axis, bit), wide)
+
+
+def scatter_pair(first, second, wide=0):
+    bits = batch_bits()
+    shape = (2,) * bits + (first.shape[0] >> bits,)
+    first, second = (part.reshape(shape + part.shape[1:]) for part in (first, second))
+    first = fold(first, "batch", 0, bits - 1)
+    second = fold(second, "batch", 1, bits - 2, wide)
+    first = fold(first, "batch", 1, bits - 2)
+    second = fold(second, "batch", 0, bits - 2, wide)
+    block = jnp.concatenate([first, second], axis=-1)
+    for bit in range(2, bits):
+        block = fold(block, "batch", bit, bits - 1 - bit, wide)
+    return block
+
+
+def columns_split(block):
+    half = block.shape[1] // 2
+    return jnp.stack([block[:, :half], block[:, half:]])
+
+
+def columns_joined(pair):
+    return jnp.concatenate([pair[0], pair[1]], axis=1)
+
+
+def both_cores(block):
+    other = exchanged(block, "stream", 0)
+    upper = lax.axis_index("stream") == 1
+    return jnp.where(upper, other, block), jnp.where(upper, block, other)
 
 
 def halved(values):
@@ -162,25 +245,59 @@
     pos_moment,
     pos_average,
 ):
-    sharded = (
-        lax.all_gather(halved(attn_weight), "batch", axis=1, tiled=True),
-        lax.all_gather(halved(up_weight), "batch", axis=0, tiled=True),
-        lax.all_gather(halved(down_weight), "batch", axis=0, tiled=True),
-        lax.all_gather(halved(layer_vectors), "batch", axis=1, tiled=True),
-        lax.all_gather(halved(up_bias)[None, :], "batch", axis=1, tiled=True),
-        lax.all_gather(halved(pos_table), "batch", axis=1, tiled=True),
-    )
-    gathered = (
-        lax.all_gather(sharded[0], "stream", axis=2, tiled=True),
-        lax.all_gather(sharded[1], "stream", axis=1, tiled=True),
-        lax.all_gather(sharded[2], "stream", axis=1, tiled=True),
-        lax.all_gather(sharded[3], "stream", axis=0, tiled=True),
-        lax.all_gather(sharded[4], "stream", axis=0, tiled=True),
-        lax.all_gather(sharded[5], "stream", axis=0, tiled=True),
-    )
-    attn_full, up_full, down_full, vector_half, bias_half, pos_full = gathered
-    vectors = vector_half.astype(jnp.float32)
-    bias_row = bias_half.reshape(-1).astype(jnp.float32)
+    rows = up_weight.shape[0]
+    live_row = (lengths[0, 0] > 0).astype(jnp.float32)
+    misc = jnp.concatenate(
+        [
+            layer_vectors.T,
+            up_bias.reshape(rows, 2),
+            jnp.broadcast_to(live_row[None, :], (rows, live_row.shape[0])),
+        ],
+        axis=1,
+    )
+    misc = jnp.pad(misc, ((0, 0), (0, 128 - misc.shape[1])))
+    entry_block = halved(
+        jnp.concatenate(
+            [attn_weight[0], attn_weight[1], attn_weight[2], pos_table.T, misc], axis=1
+        )
+    )
+    middle_block = halved(
+        jnp.concatenate(
+            [up_weight, attn_weight[3], jnp.zeros((rows, 128), jnp.float32)], axis=1
+        )
+    )
+    entry_both = both_cores(columns_joined(gather_pair(columns_split(entry_block))))
+    middle_both = both_cores(columns_joined(gather_pair(columns_split(middle_block))))
+    down_both = lax.all_gather(halved(down_weight), ("stream", "batch"), axis=0, tiled=True)
+    quarter = attn_weight.shape[2]
+    hidden_half = up_weight.shape[1]
+    attn_full = [
+        jnp.concatenate([part[:, k * quarter : (k + 1) * quarter] for part in entry_both], axis=1)
+        for k in range(3)
+    ]
+    attn_full.append(
+        jnp.concatenate(
+            [part[:, hidden_half : hidden_half + quarter] for part in middle_both], axis=1
+        )
+    )
+    up_full = jnp.concatenate([part[:, :hidden_half] for part in middle_both], axis=1)
+    down_full = jnp.concatenate(
+        [down_both[: down_both.shape[0] // 2], down_both[down_both.shape[0] // 2 :]], axis=1
+    )
+    pos_at = 3 * quarter
+    misc_at = pos_at + pos_table.shape[0]
+    pos_full = jnp.concatenate([part[:, pos_at:misc_at].T for part in entry_both], axis=0)
+    vectors = jnp.concatenate(
+        [part[:, misc_at : misc_at + 4].T for part in entry_both], axis=0
+    ).astype(jnp.float32)
+    bias_row = jnp.concatenate(
+        [part[:, misc_at + 4 : misc_at + 6].reshape(-1) for part in entry_both]
+    ).astype(jnp.float32)
+    slots_at = misc_at + 6
+    lives = [
+        part[::rows, slots_at : slots_at + live_row.shape[0]].reshape(-1) > 0
+        for part in entry_both
+    ]
     inputs = tokens[0].astype(jnp.float32)
     lengths_row = lengths[0, 0]
     token_count, width = inputs.shape
@@ -188,9 +305,13 @@
     head_size = width // HEADS
     score_scale = 1.0 / math.sqrt(head_size)
     counted, position, present, member = layout(lengths_row, token_count)
-    hidden0 = inputs + jnp.take(pos_full, position, axis=0).astype(jnp.float32)
+    long_rows = token_count // 2
+    short_rows = token_count // slot_count
+    short_tiled = jnp.tile(pos_full[:short_rows], (long_rows // short_rows, 1))
+    pos_rows = jnp.where(counted == 2, pos_full, short_tiled).astype(jnp.float32)
+    hidden0 = (inputs.reshape(2, long_rows, width) + pos_rows[None]).reshape(token_count, width)
     entry = halved(hidden0)
-    triple = jnp.einsum("td,pde->pte", entry, attn_full[:3], preferred_element_type=jnp.float32)
+    triple = [matmul(entry, attn_full[k]) for k in range(3)]
     query_half = halved(triple[0] + vectors[0]).reshape(token_count, HEADS, head_size)
     key_half = halved(triple[1]).reshape(token_count, HEADS, head_size)
     value_half = halved(triple[2] + vectors[1]).reshape(token_count, HEADS, head_size)
@@ -212,37 +333,40 @@
     pooled = jnp.dot(pool.T, hidden2, precision=lax.Precision.HIGHEST)
     inverse_norm = lax.rsqrt(jnp.sum(pooled * pooled, axis=-1, keepdims=True) + EPS_NORM)
     unit_half = halved(pooled * inverse_norm)
-    row_live = (lengths_row > 0).astype(jnp.float32)
-    live_half = halved(row_live)
     batch_index = lax.axis_index("batch")
     pair_total = lax.axis_size("batch") * slot_count
-    partner = swapped(unit_half, "stream", 0)
-    others, other_live = (
-        lax.all_gather(partner, "batch", axis=0, tiled=True),
-        lax.all_gather(live_half, "batch", axis=0, tiled=True),
-    )
-    logits = (
-        jnp.einsum("sd,md->sm", unit_half, others, preferred_element_type=jnp.float32) * INV_TEMP
-    )
-    logits = jnp.where(other_live[None, :] > 0, logits, NEGATIVE)
-    highest = jnp.max(logits, axis=-1, keepdims=True)
-    weights = jnp.exp(logits - highest)
-    probs = weights / jnp.sum(weights, axis=-1, keepdims=True)
+    units = unit_half
+    for depth, bit in enumerate(range(batch_bits() - 1, -1, -1)):
+        units = joined(
+            units, exchanged(units, "batch", bit), bit_at("batch", bit) == 1, depth
+        )
+    units = units.reshape(pair_total, width)
+    others = exchanged(units, "stream", 0)
+    upper = lax.axis_index("stream") == 1
+    own_live = jnp.where(upper, lives[1], lives[0])
+    other_live = jnp.where(upper, lives[0], lives[1])
     own_rows = batch_index * slot_count + jnp.arange(slot_count, dtype=jnp.int32)
-    target = (jnp.arange(pair_total, dtype=jnp.int32)[None, :] == own_rows[:, None]).astype(
-        jnp.float32
-    )
-    dlogit_half = halved(LOSS_WEIGHT * (probs - target) * row_live[:, None])
-    own_grad = (
-        jnp.einsum("sm,md->sd", dlogit_half, others, preferred_element_type=jnp.float32) * INV_TEMP
-    )
-    other_grad = (
-        jnp.einsum("sm,sd->md", dlogit_half, unit_half, preferred_element_type=jnp.float32)
-        * INV_TEMP
-    )
-    summed = lax.psum_scatter(other_grad, "batch", scatter_dimension=0, tiled=True)
-    returned = swapped(summed, "stream", 0)
-    dunit = own_grad + returned
+    all_rows = jnp.arange(pair_total, dtype=jnp.int32)
+    row_live = (lengths_row > 0).astype(jnp.float32)
+
+    def loss_grad(rows, columns, rows_at, rows_live, columns_live):
+        logits = (
+            jnp.einsum("sd,md->sm", rows, columns, preferred_element_type=jnp.float32) * INV_TEMP
+        )
+        logits = jnp.where(columns_live[None, :], logits, NEGATIVE)
+        highest = jnp.max(logits, axis=-1, keepdims=True)
+        weights = jnp.exp(logits - highest)
+        probs = weights / jnp.sum(weights, axis=-1, keepdims=True)
+        target = (all_rows[None, :] == rows_at[:, None]).astype(jnp.float32)
+        return halved(LOSS_WEIGHT * (probs - target) * rows_live[:, None])
+
+    dlogit_own = loss_grad(unit_half, others, own_rows, row_live, other_live)
+    dlogit_all = loss_grad(others, units, all_rows, other_live.astype(jnp.float32), own_live)
+    dlogit_in = lax.dynamic_slice_in_dim(dlogit_all, batch_index * slot_count, slot_count, 1)
+    dunit = INV_TEMP * (
+        matmul(dlogit_own, others)
+        + jnp.einsum("ms,md->sd", dlogit_in, others, preferred_element_type=jnp.float32)
+    )
     along = jnp.sum(pooled * dunit, axis=-1, keepdims=True)
     dpooled = inverse_norm * dunit - inverse_norm * inverse_norm * inverse_norm * pooled * along
     dhidden2 = jnp.dot(pool, dpooled, precision=lax.Precision.HIGHEST)
@@ -282,21 +406,20 @@
             score_scale,
         ),
     )
-    dtriple_half = halved(jnp.stack([dquery, dkey, dvalue]))
-    in_grads = jnp.einsum("td,pte->pde", entry, dtriple_half, preferred_element_type=jnp.float32)
-    dhidden0 = dresid1 + jnp.einsum(
-        "pte,pde->td", dtriple_half, attn_full[:3], preferred_element_type=jnp.float32
-    )
-    long_rows = token_count // 2
-    short_rows = token_count // slot_count
+    dtriple_half = [halved(part) for part in (dquery, dkey, dvalue)]
+    in_grads = [
+        jnp.einsum("td,te->de", entry, part, preferred_element_type=jnp.float32)
+        for part in dtriple_half
+    ]
+    dhidden0 = dresid1 + sum(
+        jnp.einsum("te,de->td", part, attn_full[k], preferred_element_type=jnp.float32)
+        for k, part in enumerate(dtriple_half)
+    )
     long_sum = jnp.sum(dhidden0.reshape(2, long_rows, width), axis=0)
-    short_sum = jnp.sum(dhidden0.reshape(slot_count, short_rows, width), axis=0)
-    short_full = jnp.concatenate(
-        [short_sum, jnp.zeros((long_rows - short_rows, width), jnp.float32)], axis=0
-    )
-    pos_row_grad = jnp.where(counted == 2, long_sum, short_full)
-    attn_term = jnp.concatenate([in_grads, out_grad[None]], axis=0)
-    vector_term = jnp.stack(
+    short_sum = jnp.sum(long_sum.reshape(-1, short_rows, width), axis=0)
+    short_full = jnp.pad(short_sum, ((0, long_rows - short_rows), (0, 0)))
+    pos_columns = jnp.where(counted == 2, long_sum, short_full).T
+    vector_columns = jnp.stack(
         [
             jnp.sum(dquery, axis=0),
             jnp.sum(dvalue, axis=0),
@@ -306,24 +429,66 @@
             dshift1,
             dgain2,
             dshift2,
-        ]
-    )
-    bias_term = jnp.sum(dpre, axis=0).reshape(lax.axis_size("stream"), -1)
-    partial_value = (
-        lax.psum_scatter(attn_term, "batch", scatter_dimension=1, tiled=True),
-        lax.psum_scatter(up_grad, "batch", scatter_dimension=0, tiled=True),
-        lax.psum_scatter(down_grad, "batch", scatter_dimension=0, tiled=True),
-        lax.psum_scatter(vector_term, "batch", scatter_dimension=1, tiled=True),
-        lax.psum_scatter(bias_term, "batch", scatter_dimension=1, tiled=True),
-        lax.psum_scatter(pos_row_grad, "batch", scatter_dimension=1, tiled=True),
+        ],
+        axis=1,
+    )
+    bias_columns = jnp.sum(dpre, axis=0).reshape(2, width, 2)
+    down_rows = down_weight.shape[0] // 2
+
+    def down_part(s):
+        part = down_grad[:, s * quarter : (s + 1) * quarter].reshape(-1, 2, down_rows, quarter)
+        return (part[:, 0].reshape(-1, quarter), part[:, 1].reshape(-1, quarter))
+
+    def middle_part(s):
+        block = jnp.concatenate(
+            [
+                up_grad[:, s * hidden_half : (s + 1) * hidden_half],
+                out_grad[:, s * quarter : (s + 1) * quarter],
+                jnp.zeros((width, 128), jnp.float32),
+            ],
+            axis=1,
+        )
+        return (block[:, : block.shape[1] // 2], block[:, block.shape[1] // 2 :])
+
+    def entry_part(s):
+        columns = [part[:, s * quarter : (s + 1) * quarter] for part in in_grads]
+        misc_grad = jnp.concatenate(
+            [
+                vector_columns[:, 4 * s : 4 * s + 4],
+                bias_columns[s],
+                jnp.zeros((width, 58), jnp.float32),
+            ],
+            axis=1,
+        )
+        pos_part = pos_columns[:, s * (long_rows // 2) : (s + 1) * (long_rows // 2)]
+        return (
+            jnp.concatenate(columns[:2], axis=1),
+            jnp.concatenate([columns[2], pos_part, misc_grad], axis=1),
+        )
+
+    def reduced(part, wide=0):
+        first, second = part(0), part(1)
+        return scatter_pair(
+            fold(jnp.stack([first[0], second[0]]), "stream", 0, 0),
+            fold(jnp.stack([first[1], second[1]]), "stream", 0, 0, wide),
+            wide,
+        )
+
+    down_sum = reduced(down_part)
+    down_sum = jnp.concatenate([down_sum[:, :quarter], down_sum[:, quarter:]], axis=0)
+    middle_sum = reduced(middle_part)
+    entry_sum = reduced(entry_part, 64)
+    attn_sum = jnp.stack(
+        [entry_sum[:, k * quarter : (k + 1) * quarter] for k in range(3)]
+        + [middle_sum[:, hidden_half : hidden_half + quarter]]
     )
     reduced = (
-        lax.psum_scatter(partial_value[0], "stream", scatter_dimension=2, tiled=True),
-        lax.psum_scatter(partial_value[1], "stream", scatter_dimension=1, tiled=True),
-        lax.psum_scatter(partial_value[2], "stream", scatter_dimension=1, tiled=True),
-        lax.psum_scatter(partial_value[3], "stream", scatter_dimension=0, tiled=True),
-        lax.psum_scatter(partial_value[4], "stream", scatter_dimension=0, tiled=True),
-        lax.psum_scatter(partial_value[5], "stream", scatter_dimension=0, tiled=True),
+        attn_sum,
+        middle_sum[:, :hidden_half],
+        down_sum,
+        entry_sum[:, misc_at : misc_at + 4].T,
+        entry_sum[:, misc_at + 4 : misc_at + 6].reshape(-1),
+        entry_sum[:, pos_at:misc_at].T,
     )
     attn_all = renew(reduced[0], attn_moment, attn_weight, attn_average, RATE)
     up_all = renew(reduced[1], up_moment, up_weight, up_average, RATE)

time: 1810 us -> 676 us (0.37)
  waiting for transfers between devices: 1200 us -> 110 us
  blocking collectives: 162 us -> 0 us
  starting transfers between devices: 1.1 us -> 146 us
  matrix products: 192 us -> 113 us
  other arithmetic: 64.8 us -> 98.3 us
    unnamed x22 -> x1, waiting for transfers between devices: 617 us -> 0.02 us
    reduce_scatter x6 -> x0, waiting for transfers between devices: 449 us -> none  [the longest x1 173 us: local(): lax.psum_scatter(down_grad, 'batch', scatter_dimension=0, tiled=True)]
    ppermute x2 -> x43, starting transfers between devices: 0.2 us -> 145 us  [exchanged(): return lax.ppermute(block, axis, route)]
    all_gather x6 -> x1, waiting for transfers between devices: 128 us -> 0.02 us  [local(): lax.all_gather(halved(down_weight), ('stream', 'batch'), axis=0, tiled=True)]
    all_gather x6 -> x0, blocking collectives: 122 us -> none  [the longest x1 42 us: local(): lax.all_gather(halved(pos_table), 'batch', axis=1, tiled=True)]
    ppermute x2 -> x43, waiting for transfers between devices: 2.39 us -> 110 us  [exchanged(): return lax.ppermute(block, axis, route)]
    unnamed x2 -> x0, blocking collectives: 40.1 us -> none
    unnamed x146 -> x299, local copies, waits for them, and re-layouts: 67.2 us -> 31.5 us
  transfers between devices with their start and end apart: 19 -> 44, of which waited for: 13 -> 20; matrix products, arithmetic and copies ran while one was open for 11% -> 24% of each run, Pallas kernels for 0% -> 0%
where the time goes in v1:
time: 676 us; the launch traced here: 665 us
  local copies, waits for them, and re-layouts  159 us (24%)
  starting transfers between devices  146 us (22%)
  matrix products  113 us (17%)
  waiting for transfers between devices  110 us (16%)
  other arithmetic  98.3 us (15%)
  between operations  19.7 us (3%)
  loops' own time  19.1 us (3%)
    ppermute x43, starting transfers between devices, exchanged(): return lax.ppermute(block, axis, route)  145 us
    ppermute x43, waiting for transfers between devices, exchanged(): return lax.ppermute(block, axis, route)  110 us
    another operation x37, local copies, waits for them, and re-layouts  34.3 us
    unnamed x299, local copies, waits for them, and re-layouts  31.5 us
    dot_general x7, matrix products, matmul(): return jnp.dot(left, right, preferred_element_type=jnp.float32)  24.6 us
    add x24, other arithmetic, fold(): return kept + unpacked(exchanged(sent, axis, bit), wide)  24.3 us
    unnamed x2, loops' own time  19.1 us
    concatenate x2, local copies, waits for them, and re-layouts, entry_part(): jnp.concatenate([columns[2], pos_part, misc_grad], axis=1)  18.6 us
  transfers between devices with their start and end apart: 44, of which 20 were waited for; matrix products, arithmetic and copies ran while one was open for 24% of the time, Pallas kernels for 0%

profile of v1, /device:TPU:0, one launch (start us, length us, event | category | flops | bytes accessed | tf_op | source)
XLA Modules:
  0.0 665.0 jit_solution(13154710206999538561)
XLA Ops:
  11.6 4.1 collective-permute-start
  17.5 10.2 %collective-permute-done = bf16[2,48,768]{2,1,0:T(8,128)(2,1)S(1)} collective-permute-done((bf16[2,48,768]{2,1,0:T(8,128)(2,1)S(1)}, bf16[2,48,768]{2,1,0:T(8,128)(2,1)S(1)}, u32[]{:S(2)}, u32[]{:S(2)}) %collective-permute-start) | collective-permute-done | bytes 147488 | tf_op jit(solution)/shard_map/ppermute | solution.py:26
  31.0 9.1 %collective-permute-done.1 = bf16[2,2,48,768]{3,2,0,1:T(8,128)(2,1)S(1)} collective-permute-done((bf16[2,2,48,768]{3,2,0,1:T(8,128)(2,1)S(1)}, bf16[2,2,48,768]{3,2,0,1:T(8,128)(2,1)S(1)}, u32[]{:S(2)}, u32[]{:S(2)}) %collective-permute-start.1) | collective-permute-done | bytes 294944 | tf_op jit(solution)/shard_map/ppermute | solution.py:26
  43.7 6.7 %collective-permute-done.2 = bf16[2,2,48,768]{3,2,1,0:T(8,128)(2,1)S(1)} collective-permute-done((bf16[2,2,48,768]{3,2,1,0:T(8,128)(2,1)S(1)}, bf16[2,2,48,768]{3,2,1,0:T(8,128)(2,1)S(1)}, u32[]{:S(2)}, u32[]{:S(2)}) %collective-permute-start.2) | collective-permute-done | bytes 294944 | tf_op jit(solution)/shard_map/ppermute | solution.py:26
  52.2 3.2 collective-permute-done.4
  61.8 6.9 %collective-permute-done.3 = bf16[2,2,2,48,768]{4,3,2,1,0:T(8,128)(2,1)S(1)} collective-permute-done((bf16[2,2,2,48,768]{4,3,2,1,0:T(8,128)(2,1)S(1)}, bf16[2,2,2,48,768]{4,3,2,1,0:T(8,128)(2,1)S(1)}, u32[]{:S(2)}, u32[]{:S(2)}) %collective-permute-start.3) | collective-permute-done | bytes 589856 | tf_op jit(solution)/shard_map/ppermute | solution.py:26
  69.6 4.3 collective-permute-done.5
  76.4 7.4 %collective-permute-done.11 = bf16[2,2,48,1024]{3,2,1,0:T(8,128)(2,1)} collective-permute-done((bf16[2,2,48,1024]{3,2,1,0:T(8,128)(2,1)}, bf16[2,2,48,1024]{3,2,1,0:T(8,128)(2,1)}, u32[]{:S(2)}, u32[]{:S(2)}) %collective-permute-start.11) | collective-permute-done | bytes 393248 | tf_op jit(solution)/shard_map/ppermute | solution.py:26
  91.5 11.4 %collective-permute-done.12 = bf16[2,2,2,48,1024]{4,3,1,0,2:T(8,128)(2,1)} collective-permute-done((bf16[2,2,2,48,1024]{4,3,1,0,2:T(8,128)(2,1)}, bf16[2,2,2,48,1024]{4,3,1,0,2:T(8,128)(2,1)}, u32[]{:S(2)}, u32[]{:S(2)}) %collective-permute-start.12) | collective-permute-done | bytes 786464 | tf_op jit(solution)/shard_map/ppermute | solution.py:26
  108.9 4.0 broadcast_select_fusion.3
  123.5 2.7 add_convert_fusion.1
  126.2 27.6 %conditional.6 = (f32[1024,12]{1,0:T(8,128)S(1)}, bf16[1024,768]{0,1:T(8,128)(2,1)S(1)}) conditional(s32[]{:T(128)} %convert_element_type.373, (pred[1024]{0:T(1024)(128)(4,1)S(1)}, bf16[1024,768]{1,0:T(8,128)(2,1)}, bf16[1024,768]{1,0:T(8,128)(2,1)S(1)}, bf16[1024,768]{1,0:T(8,128)(2,1)S(1)}) %tuple.60, (pred[1024]{0:T(1024)(128)(4,1)S(1)}, ...), branch_computations={%region_2.7_spmd, %region_5.10_spmd} | conditional | flops 1686884352 | bytes 113742896
  126.4 2.6 copy.754
  129.0 3.0 copy.820
  141.5 4.5 fusion.9
  153.8 4.3 broadcast_select_fusion.1
  165.1 10.9 %multiply_convert_fusion.4 = (bf16[1024,3072]{1,0:T(8,128)(2,1)}, f32[1024,3072]{1,0:T(8,128)}) fusion(f32[3072]{0:T(1024)S(1)} %maximum_convert_fusion.1, bf16[768,1536]{1,0:T(8,128)(2,1)S(1)} %slice.511, bf16[768,1536]{1,0:T(8,128)(2,1)S(1)} %slice.510, f32[1024,768]{1,0:T(8,128)S(1)} %get-tuple-element.734, f32[768]{0:T(1024)S(1)} %get-tuple-element.577, ...), kind=kOutput, calls=%fused_computation.92 | convolution fusion | flops 4864081920 | bytes 26765312 | tf_op jit(solution)/shard_map/dot_general | solution.py:121
  176.0 3.0 fusion.242
  180.7 5.4 fusion.253
  189.7 37.5 %collective-permute-start.14 = (bf16[8,768]{1,0:T(8,128)(2,1)S(1)}, bf16[8,768]{1,0:T(8,128)(2,1)S(1)}, u32[]{:S(2)}, u32[]{:S(2)}) collective-permute-start(bf16[8,768]{1,0:T(8,128)(2,1)S(1)} %multiply_convert_fusion.5), channel_id=1, source_target_pairs={{0,8},{1,9},{2,10},{3,11},{4,12},{5,13},{6,14},{7,15},{8,0},{9,1},... | collective-permute-start | bytes 36872 | tf_op jit(solution)/shard_map/ppermute | solution.py:26
  229.6 3.2 collective-permute-done.15
  237.4 3.5 collective-permute-start.17
  247.1 7.2 %multiply_reduce_fusion.2 = (f32[768]{0:T(1024)}, f32[1024]{0:T(1024)S(1)}, f32[1024]{0:T(1024)S(1)}, f32[768]{0:T(1024)}, f32[1024,768]{1,0:T(8,128)S(1)}) fusion(f32[1024,768]{1,0:T(8,128)} %copy-done.1, f32[1024]{0:T(1024)S(1)} %copy-done.122, f32[1024]{0:T(1024)S(1)} %broadcast_multiply_fusion.4, f32[768]{0:T(1024)S(1)} %get-tuple-element.574, ...), kind=kOutput, calls=%fused_computation.143 | convolution fusion | flops 82620928 | bytes 6371456 | tf_op jit(solution)/shard_map/dot_general | solution.py:372
  254.3 3.2 fusion.235
  257.5 7.7 %fusion.140 = f32[3072,768]{1,0:T(8,128)} fusion(bf16[1024,3072]{1,0:T(8,128)(2,1)S(1)} %bitcast.559, f32[1024,768]{1,0:T(8,128)S(1)} %get-tuple-element.604), kind=kOutput, calls=%fused_computation.271 | convolution fusion | flops 4832624640 | bytes 18874368 | tf_op jit(solution)/shard_map/tf,td->fd/dot_general | solution.py:375
  265.3 12.5 %fusion.256 = (f32[3072]{0:T(1024)}, bf16[1024,3072]{1,0:T(8,128)(2,1)S(1)}) fusion(f32[1024,3072]{1,0:T(8,128)} %get-tuple-element.736, f32[3072]{0:T(1024)S(1)} %copy-done.130, bf16[3072,384]{1,0:T(8,128)(2,1)S(1)} %copy-done.84, bf16[3072,384]{1,0:T(8,128)(2,1)S(1)} %copy-done.82, f32[1024,768]{1,0:T(8,128)S(1)} %get-tuple-element.604), kind=kOutput, calls=%fused_computation.553 | convolution fusion | flops 4879807488 | bytes 26763264 | tf_op jit(solution)/shard_map/td,fd->tf/dot_general | solution.py:378
  277.8 6.5 multiply_reduce_fusion.3
  286.2 2.6 convolution_convert_fusion
  288.8 60.8 %conditional.7 = (f32[768,1]{0,1:T(1,128)S(1)}, f32[768,1]{0,1:T(1,128)S(1)}, bf16[1024,768]{0,1:T(8,128)(2,1)}, bf16[1024,768]{0,1:T(8,128)(2,1)}, bf16[1024,768]{0,1:T(8,128)(2,1)}) conditional(s32[]{:T(128)} %convert_element_type.373, (pred[1024]{0:T(1024)(128)(4,1)S(1)}, bf16[1024,768]{1,0:T(8,128)(2,1)}, bf16[1024,768]{1,0:T(8,128)(2,1)}, ...), branch_computations={%region_22.30_spmd, %region_26.34_spmd} | conditional | flops 4127181312 | bytes 318086272
  288.8 2.7 copy.771
  291.5 3.0 copy.825
  294.5 2.6 copy.770
  299.1 3.7 fusion.41
  304.1 2.6 copy.773
  306.7 3.1 copy.827
  309.8 2.6 copy.774
  314.4 5.2 multiply_reduce_fusion
  325.5 2.8 bitcast_reduce_fusion
  329.5 2.7 copy_bitcast_fusion.1
  349.7 3.3 fusion.143
  354.9 2.8 fusion.259
  357.8 3.2 add_add_fusion
  361.0 3.5 reduce_sum.295
  379.2 9.8 %concatenate.155 = f32[768,704]{0,1:T(8,128)} concatenate(f32[768,384]{0,1:T(8,128)} %get-tuple-element.646, f32[768,256]{0,1:T(8,128)} %get-tuple-element.662, f32[768,1]{0,1:T(1,128)} %stack.316, f32[768,1]{0,1:T(1,128)} %stack.317, f32[768,1]{0,1:T(1,128)} %stack.318, f32[768,1]{0,1:T(1,128)} %stack.319, f32[768,2]{0,1:T(2,128)} %copy.782, f32[768,58]{0,1:T(8,128)S(1)} %broadcast.305), dimensions={1} | concatenate | bytes 4325376 | tf_op jit(solution)/shard_map/concatenate | solution.py:466
  389.0 8.9 %concatenate.154 = f32[768,704]{0,1:T(8,128)} concatenate(f32[768,384]{0,1:T(8,128)} %get-tuple-element.647, f32[768,256]{0,1:T(8,128)} %get-tuple-element.663, f32[768,1]{0,1:T(1,128)S(1)} %copy-done.133, f32[768,1]{0,1:T(1,128)S(1)} %copy-done.135, f32[768,1]{0,1:T(1,128)S(1)} %copy-done.131, f32[768,1]{0,1:T(1,128)S(1)} %stack.314, f32[768,2]{0,1:T(2,128)S(1)} %copy-done.125, ...), dimensions={1} | concatenate | bytes 4325376 | tf_op jit(solution)/shard_map/concatenate | solution.py:466
  397.8 4.3 fusion.111
  403.5 2.8 fusion.257
  406.3 2.8 fusion.258
  409.1 2.9 fusion.137
  412.0 8.3 %fusion.86 = f32[768,3072]{1,0:T(8,128)} fusion(bf16[1024,3072]{1,0:T(8,128)(2,1)S(1)} %bitcast.498, f32[1024,768]{1,0:T(8,128)S(1)} %get-tuple-element.734, f32[768]{0:T(1024)S(1)} %copy-done.118, f32[768]{0:T(1024)S(1)} %get-tuple-element.578, f32[1024]{0:T(1024)S(1)} %add_rsqrt_fusion.1, f32[1024]{0:T(1024)S(1)} %broadcast_multiply_fusion.5), kind=kOutput, calls=%fused_computation.148 | convolution fusion | flops 4835770368 | bytes 18888704 | tf_op jit(solution)/shard_map/td,tf->df/dot_general | solution.py:381
  420.4 4.4 fusion.238
  443.0 4.5 fusion.239
  462.0 65.6 %collective-permute-start.39 = (bf16[2,2,2,96,384]{4,3,1,0,2:T(8,128)(2,1)}, bf16[2,2,2,96,384]{4,3,1,0,2:T(8,128)(2,1)}, u32[]{:S(2)}, u32[]{:S(2)}) collective-permute-start(bf16[2,2,2,96,384]{4,3,1,0,2:T(8,128)(2,1)} %fusion.147), channel_id=1, source_target_pairs={{0,2},{1,3},{2,0},{3,1},{4,6},{5,7},{6,4},{7,5},{8,10},{9,11},{10,... | collective-permute-start | bytes 1769480 | tf_op jit(solution)/shard_map/ppermute | solution.py:26
  533.1 2.6 slice.531
  535.8 2.9 copy.784
  548.0 3.0 fusion.109
  551.1 3.3 copy.780
  556.1 3.4 fusion.73
  576.2 19.1 %collective-permute-done.40 = bf16[2,2,96,384]{3,2,1,0:T(8,128)(2,1)S(1)} collective-permute-done((bf16[2,2,96,384]{3,2,1,0:T(8,128)(2,1)S(1)}, bf16[2,2,96,384]{3,2,1,0:T(8,128)(2,1)S(1)}, u32[]{:S(2)}, u32[]{:S(2)}) %collective-permute-start.40) | collective-permute-done | bytes 294944 | tf_op jit(solution)/shard_map/ppermute | solution.py:26
  597.2 3.0 collective-permute-done.24
  605.4 3.2 collective-permute-start.42
  608.6 4.8 collective-permute-done.25
  641.0 5.5 collective-permute-done.33
  649.3 6.1 collective-permute-done.34
  (653 shorter events, 223.4 us)
Async XLA Ops:
  7.2 20.7 %copy-start.142 = (s32[1,1,8]{2,1,0:T(1,128)S(1)}, s32[1,1,8]{2,1,0:T(1,128)}, u32[]{:S(2)}) copy-start(s32[1,1,8]{2,1,0:T(1,128)} %param.33) | copy-start | bytes 100
  7.2 168.8 %all-gather.2.cloned.1.call-start = ((), (), s32[]{:S(2)}) async-start(), calls=%async_computation | async-start | bytes 4866048 | tf_op jit(solution)/shard_map/all_gather | solution.py:271
  11.6 16.2 %collective-permute-start = (bf16[2,48,768]{2,1,0:T(8,128)(2,1)S(1)}, bf16[2,48,768]{2,1,0:T(8,128)(2,1)S(1)}, u32[]{:S(2)}, u32[]{:S(2)}) collective-permute-start(bf16[2,48,768]{2,1,0:T(8,128)(2,1)S(1)} %pad_maximum_fusion.46), channel_id=1, source_target_pairs={{0,8},{1,9},{2,10},{3,11},{4,12},{5,13},{6,14},{7,15},{8,0},{9,1},... | collective-permute-start | bytes 442376 | tf_op jit(solution)/shard_map/ppermute | solution.py:26
  16.7 25.3 %collective-permute-start.7 = (bf16[2,48,1024]{2,1,0:T(8,128)(2,1)S(1)}, bf16[2,48,1024]{2,1,0:T(8,128)(2,1)S(1)}, u32[]{:S(2)}, u32[]{:S(2)}) collective-permute-start(bf16[2,48,1024]{2,1,0:T(8,128)(2,1)S(1)} %pad_maximum_fusion.44), channel_id=1, source_target_pairs={{0,8},{1,9},{2,10},{3,11},{4,12},{5,13},{6,14},{7,15},{8,0},{9,1},... | collective-permute-start | bytes 589832 | tf_op jit(solution)/shard_map/ppermute | solution.py:26
  27.8 12.3 %collective-permute-start.1 = (bf16[2,2,48,768]{3,2,0,1:T(8,128)(2,1)S(1)}, bf16[2,2,48,768]{3,2,0,1:T(8,128)(2,1)S(1)}, u32[]{:S(2)}, u32[]{:S(2)}) collective-permute-start(bf16[2,2,48,768]{3,2,0,1:T(8,128)(2,1)S(1)} %pad_maximum_fusion.39), channel_id=1, source_target_pairs={{0,4},{1,5},{2,6},{3,7},{4,0},{5,1},{6,2},{7,3},{8,12},{9,13},{10,... | collective-permute-start | bytes 884744 | tf_op jit(solution)/shard_map/ppermute | solution.py:26
  40.2 10.3 %collective-permute-start.2 = (bf16[2,2,48,768]{3,2,1,0:T(8,128)(2,1)S(1)}, bf16[2,2,48,768]{3,2,1,0:T(8,128)(2,1)S(1)}, u32[]{:S(2)}, u32[]{:S(2)}) collective-permute-start(bf16[2,2,48,768]{3,2,1,0:T(8,128)(2,1)S(1)} %get-tuple-element.694), channel_id=1, source_target_pairs={{0,2},{1,3},{2,0},{3,1},{4,6},{5,7},{6,4},{7,5},{8,10},{9,11},{10,... | collective-permute-start | bytes 884744 | tf_op jit(solution)/shard_map/ppermute | solution.py:26
  42.1 14.2 %collective-permute-start.8 = (bf16[2,2,48,1024]{3,2,0,1:T(8,128)(2,1)S(1)}, bf16[2,2,48,1024]{3,2,0,1:T(8,128)(2,1)S(1)}, u32[]{:S(2)}, u32[]{:S(2)}) collective-permute-start(bf16[2,2,48,1024]{3,2,0,1:T(8,128)(2,1)S(1)} %pad_maximum_fusion.37), channel_id=1, source_target_pairs={{0,4},{1,5},{2,6},{3,7},{4,0},{5,1},{6,2},{7,3},{8,12},{9,13},{10,... | collective-permute-start | bytes 1179656 | tf_op jit(solution)/shard_map/ppermute | solution.py:26
  42.2 13.2 %collective-permute-start.4 = (bf16[2,2,48,768]{3,2,1,0:T(8,128)(2,1)S(1)}, bf16[2,2,48,768]{3,2,1,0:T(8,128)(2,1)S(1)}, u32[]{:S(2)}, u32[]{:S(2)}) collective-permute-start(bf16[2,2,48,768]{3,2,1,0:T(8,128)(2,1)S(1)} %get-tuple-element.695), channel_id=1, source_target_pairs={{0,1},{1,0},{2,3},{3,2},{4,5},{5,4},{6,7},{7,6},{8,9},{9,8},{10,11... | collective-permute-start | bytes 884744 | tf_op jit(solution)/shard_map/ppermute | solution.py:26
  50.6 18.1 %collective-permute-start.3 = (bf16[2,2,2,48,768]{4,3,2,1,0:T(8,128)(2,1)S(1)}, bf16[2,2,2,48,768]{4,3,2,1,0:T(8,128)(2,1)S(1)}, u32[]{:S(2)}, u32[]{:S(2)}) collective-permute-start(bf16[2,2,2,48,768]{4,3,2,1,0:T(8,128)(2,1)S(1)} %pad_maximum_fusion.33), channel_id=1, source_target_pairs={{0,1},{1,0},{2,3},{3,2},{4,5},{5,4},{6,7},{7,6},{8,9},{9,8},{10,11... | collective-permute-start | bytes 1769480 | tf_op jit(solution)/shard_map/ppermute | solution.py:26
  56.3 17.6 %collective-permute-start.5 = (bf16[2,2,2,48,768]{4,3,1,0,2:T(8,128)(2,1)}, bf16[2,2,2,48,768]{4,3,1,0,2:T(8,128)(2,1)S(1)}, u32[]{:S(2)}, u32[]{:S(2)}) collective-permute-start(bf16[2,2,2,48,768]{4,3,1,0,2:T(8,128)(2,1)} %pad_maximum_fusion.34), channel_id=1, source_target_pairs={{0,2},{1,3},{2,0},{3,1},{4,6},{5,7},{6,4},{7,5},{8,10},{9,11},{10,... | collective-permute-start | bytes 1769480 | tf_op jit(solution)/shard_map/ppermute | solution.py:26
  57.3 28.8 %collective-permute-start.9 = (bf16[2,2,48,1024]{3,2,1,0:T(8,128)(2,1)}, bf16[2,2,48,1024]{3,2,1,0:T(8,128)(2,1)}, u32[]{:S(2)}, u32[]{:S(2)}) collective-permute-start(bf16[2,2,48,1024]{3,2,1,0:T(8,128)(2,1)} %get-tuple-element.677), channel_id=1, source_target_pairs={{0,2},{1,3},{2,0},{3,1},{4,6},{5,7},{6,4},{7,5},{8,10},{9,11},{10,... | collective-permute-start | bytes 1179656 | tf_op jit(solution)/shard_map/ppermute | solution.py:26
  59.3 24.6 %collective-permute-start.11 = (bf16[2,2,48,1024]{3,2,1,0:T(8,128)(2,1)}, bf16[2,2,48,1024]{3,2,1,0:T(8,128)(2,1)}, u32[]{:S(2)}, u32[]{:S(2)}) collective-permute-start(bf16[2,2,48,1024]{3,2,1,0:T(8,128)(2,1)} %get-tuple-element.678), channel_id=1, source_target_pairs={{0,1},{1,0},{2,3},{3,2},{4,5},{5,4},{6,7},{7,6},{8,9},{9,8},{10,11... | collective-permute-start | bytes 1179656 | tf_op jit(solution)/shard_map/ppermute | solution.py:26
  76.4 32.5 %collective-permute-start.6 = (bf16[768,1536]{0,1:T(8,128)(2,1)}, bf16[768,1536]{0,1:T(8,128)(2,1)}, u32[]{:S(2)}, u32[]{:S(2)}) collective-permute-start(bf16[768,1536]{0,1:T(8,128)(2,1)} %pad_maximum_fusion.9), channel_id=1, source_target_pairs={{0,16},{16,0},{1,17},{17,1},{2,18},{18,2},{3,19},{19,3},{4,20},{20... | collective-permute-start | bytes 7077896 | tf_op jit(solution)/shard_map/ppermute | solution.py:26
  86.0 16.8 %collective-permute-start.12 = (bf16[2,2,2,48,1024]{4,3,1,0,2:T(8,128)(2,1)}, bf16[2,2,2,48,1024]{4,3,1,0,2:T(8,128)(2,1)}, u32[]{:S(2)}, u32[]{:S(2)}) collective-permute-start(bf16[2,2,2,48,1024]{4,3,1,0,2:T(8,128)(2,1)} %pad_maximum_fusion.24), channel_id=1, source_target_pairs={{0,2},{1,3},{2,0},{3,1},{4,6},{5,7},{6,4},{7,5},{8,10},{9,11},{10,... | collective-permute-start | bytes 2359304 | tf_op jit(solution)/shard_map/ppermute | solution.py:26
  88.2 17.2 %collective-permute-start.10 = (bf16[2,2,2,48,1024]{4,3,2,1,0:T(8,128)(2,1)}, bf16[2,2,2,48,1024]{4,3,2,1,0:T(8,128)(2,1)}, u32[]{:S(2)}, u32[]{:S(2)}) collective-permute-start(bf16[2,2,2,48,1024]{4,3,2,1,0:T(8,128)(2,1)} %pad_maximum_fusion.23), channel_id=1, source_target_pairs={{0,1},{1,0},{2,3},{3,2},{4,5},{5,4},{6,7},{7,6},{8,9},{9,8},{10,11... | collective-permute-start | bytes 2359304 | tf_op jit(solution)/shard_map/ppermute | solution.py:26
  90.6 13.7 %copy-start.123 = (s32[1024]{0:T(1024)}, s32[1024]{0:T(1024)S(1)}, u32[]{:S(2)}) copy-start(s32[1024]{0:T(1024)S(1)} %add_select_fusion) | copy-start | bytes 12292
  108.9 44.9 %collective-permute-start.13 = (bf16[768,2048]{1,0:T(8,128)(2,1)}, bf16[768,2048]{1,0:T(8,128)(2,1)}, u32[]{:S(2)}, u32[]{:S(2)}) collective-permute-start(bf16[768,2048]{1,0:T(8,128)(2,1)} %pad_maximum_fusion.4), channel_id=1, source_target_pairs={{0,16},{16,0},{1,17},{17,1},{2,18},{18,2},{3,19},{19,3},{4,20},{20... | collective-permute-start | bytes 9437192 | tf_op jit(solution)/shard_map/ppermute | solution.py:26
  120.3 58.8 %copy-start.117 = (f32[768]{0:T(1024)}, f32[768]{0:T(1024)S(1)}, u32[]{:S(2)}) copy-start(f32[768]{0:T(1024)S(1)} %get-tuple-element.577) | copy-start | bytes 9220
  153.8 11.3 %copy-start.129 = (f32[3072]{0:T(1024)}, f32[3072]{0:T(1024)S(1)}, u32[]{:S(2)}) copy-start(f32[3072]{0:T(1024)S(1)} %maximum_convert_fusion.1) | copy-start | bytes 36868
  186.7 46.7 %copy-start.116 = (f32[256,48]{0,1:T(8,128)S(1)}, f32[256,48]{0,1:T(8,128)}, u32[]{:S(2)}) copy-start(f32[256,48]{0,1:T(8,128)} %param.49) | copy-start | bytes 147460
  186.7 47.5 %copy-start.119 = (f32[256,48]{0,1:T(8,128)S(1)}, f32[256,48]{0,1:T(8,128)}, u32[]{:S(2)}) copy-start(f32[256,48]{0,1:T(8,128)} %param.50) | copy-start | bytes 147460
  186.7 48.2 %copy-start.120 = (f32[256,48]{0,1:T(8,128)S(1)}, f32[256,48]{0,1:T(8,128)}, u32[]{:S(2)}) copy-start(f32[256,48]{0,1:T(8,128)} %param.51) | copy-start | bytes 147460
  189.7 39.1 %collective-permute-start.14 = (bf16[8,768]{1,0:T(8,128)(2,1)S(1)}, bf16[8,768]{1,0:T(8,128)(2,1)S(1)}, u32[]{:S(2)}, u32[]{:S(2)}) collective-permute-start(bf16[8,768]{1,0:T(8,128)(2,1)S(1)} %multiply_convert_fusion.5), channel_id=1, source_target_pairs={{0,8},{1,9},{2,10},{3,11},{4,12},{5,13},{6,14},{7,15},{8,0},{9,1},... | collective-permute-start | bytes 36872 | tf_op jit(solution)/shard_map/ppermute | solution.py:26
  229.0 3.9 collective-permute-start.15
  232.8 4.6 collective-permute-start.16
  235.0 12.1 %copy-start.122 = (f32[1024]{0:T(1024)S(1)}, f32[1024]{0:T(1024)}, u32[]{:S(2)}) copy-start(f32[1024]{0:T(1024)} %copy-done.121) | copy-start | bytes 12292
  237.4 6.1 collective-permute-start.17
  243.7 1.5 collective-permute-start.18
  265.3 12.6 %copy-start.75 = (bf16[768,1536]{1,0:T(8,128)(2,1)S(1)}, bf16[768,1536]{1,0:T(8,128)(2,1)}, u32[]{:S(2)}) copy-start(bf16[768,1536]{1,0:T(8,128)(2,1)} %copy-done.74) | copy-start | bytes 7077892
  265.3 12.5 %copy-start.77 = (bf16[768,1536]{1,0:T(8,128)(2,1)S(1)}, bf16[768,1536]{1,0:T(8,128)(2,1)}, u32[]{:S(2)}) copy-start(bf16[768,1536]{1,0:T(8,128)(2,1)} %copy-done.76) | copy-start | bytes 7077892
  368.4 10.8 %copy-start.127 = (f32[768]{0:T(1024)S(1)}, f32[768]{0:T(1024)}, u32[]{:S(2)}) copy-start(f32[768]{0:T(1024)} %get-tuple-element.603) | copy-start | bytes 9220
  429.0 28.9 %collective-permute-start.38 = (bf16[1536,384]{1,0:T(8,128)(2,1)}, bf16[1536,384]{1,0:T(8,128)(2,1)}, u32[]{:S(2)}, u32[]{:S(2)}) collective-permute-start(bf16[1536,384]{1,0:T(8,128)(2,1)} %fusion.125), channel_id=1, source_target_pairs={{0,16},{16,0},{1,17},{17,1},{2,18},{18,2},{3,19},{19,3},{4,20},{20... | collective-permute-start | bytes 3538952 | tf_op jit(solution)/shard_map/ppermute | solution.py:26
  430.6 31.4 %collective-permute-start.35 = (bf16[1536,384]{1,0:T(8,128)(2,1)}, bf16[1536,384]{1,0:T(8,128)(2,1)}, u32[]{:S(2)}, u32[]{:S(2)}) collective-permute-start(bf16[1536,384]{1,0:T(8,128)(2,1)} %fusion.124), channel_id=1, source_target_pairs={{0,16},{16,0},{1,17},{17,1},{2,18},{18,2},{3,19},{19,3},{4,20},{20... | collective-permute-start | bytes 3538952 | tf_op jit(solution)/shard_map/ppermute | solution.py:26
  432.0 99.6 %collective-permute-start.22 = (bf16[768,768]{0,1:T(8,128)(2,1)}, bf16[768,768]{0,1:T(8,128)(2,1)}, u32[]{:S(2)}, u32[]{:S(2)}) collective-permute-start(bf16[768,768]{0,1:T(8,128)(2,1)} %pad_maximum_fusion.22), channel_id=1, source_target_pairs={{0,16},{16,0},{1,17},{17,1},{2,18},{18,2},{3,19},{19,3},{4,20},{20... | collective-permute-start | bytes 3538952 | tf_op jit(solution)/shard_map/ppermute | solution.py:26
  440.7 105.3 %collective-permute-start.19 = (bf16[768,768]{0,1:T(8,128)(2,1)}, bf16[768,768]{0,1:T(8,128)(2,1)}, u32[]{:S(2)}, u32[]{:S(2)}) collective-permute-start(bf16[768,768]{0,1:T(8,128)(2,1)} %fusion.123), channel_id=1, source_target_pairs={{0,16},{16,0},{1,17},{17,1},{2,18},{18,2},{3,19},{19,3},{4,20},{20... | collective-permute-start | bytes 3538952 | tf_op jit(solution)/shard_map/ppermute | solution.py:26
  452.8 103.0 %collective-permute-start.30 = (bf16[768,1024]{1,0:T(8,128)(2,1)}, bf16[768,1024]{1,0:T(8,128)(2,1)}, u32[]{:S(2)}, u32[]{:S(2)}) collective-permute-start(bf16[768,1024]{1,0:T(8,128)(2,1)} %fusion.118), channel_id=1, source_target_pairs={{0,16},{16,0},{1,17},{17,1},{2,18},{18,2},{3,19},{19,3},{4,20},{20... | collective-permute-start | bytes 4718600 | tf_op jit(solution)/shard_map/ppermute | solution.py:26
  457.9 102.7 %collective-permute-start.27 = (bf16[768,1024]{1,0:T(8,128)(2,1)}, bf16[768,1024]{1,0:T(8,128)(2,1)}, u32[]{:S(2)}, u32[]{:S(2)}) collective-permute-start(bf16[768,1024]{1,0:T(8,128)(2,1)} %fusion.117), channel_id=1, source_target_pairs={{0,16},{16,0},{1,17},{17,1},{2,18},{18,2},{3,19},{19,3},{4,20},{20... | collective-permute-start | bytes 4718600 | tf_op jit(solution)/shard_map/ppermute | solution.py:26
  459.2 68.5 %copy-start.17 = (f32[16,1,96,384]{3,2,1,0:T(8,128)S(1)}, f32[16,1,96,384]{3,2,1,0:T(8,128)}, u32[]{:S(2)}) copy-start(f32[16,1,96,384]{3,2,1,0:T(8,128)} %copy-done.16) | copy-start | bytes 7077892
  459.2 68.5 %copy-start.19 = (f32[16,1,96,384]{3,2,1,0:T(8,128)S(1)}, f32[16,1,96,384]{3,2,1,0:T(8,128)}, u32[]{:S(2)}) copy-start(f32[16,1,96,384]{3,2,1,0:T(8,128)} %copy-done.18) | copy-start | bytes 7077892
  461.0 68.3 %copy-start.46 = (f32[1536,384]{1,0:T(8,128)}, f32[1536,384]{1,0:T(8,128)S(1)}, u32[]{:S(2)}) copy-start(f32[1536,384]{1,0:T(8,128)S(1)} %fusion.99) | copy-start | bytes 7077892
  462.0 103.7 %collective-permute-start.39 = (bf16[2,2,2,96,384]{4,3,1,0,2:T(8,128)(2,1)}, bf16[2,2,2,96,384]{4,3,1,0,2:T(8,128)(2,1)}, u32[]{:S(2)}, u32[]{:S(2)}) collective-permute-start(bf16[2,2,2,96,384]{4,3,1,0,2:T(8,128)(2,1)} %fusion.147), channel_id=1, source_target_pairs={{0,2},{1,3},{2,0},{3,1},{4,6},{5,7},{6,4},{7,5},{8,10},{9,11},{10,... | collective-permute-start | bytes 1769480 | tf_op jit(solution)/shard_map/ppermute | solution.py:26
  531.6 37.3 %collective-permute-start.36 = (bf16[2,2,2,96,384]{4,3,2,1,0:T(8,128)(2,1)}, bf16[2,2,2,96,384]{4,3,2,1,0:T(8,128)(2,1)}, u32[]{:S(2)}, u32[]{:S(2)}) collective-permute-start(bf16[2,2,2,96,384]{4,3,2,1,0:T(8,128)(2,1)} %fusion.146), channel_id=1, source_target_pairs={{0,1},{1,0},{2,3},{3,2},{4,5},{5,4},{6,7},{7,6},{8,9},{9,8},{10,11... | collective-permute-start | bytes 1769480 | tf_op jit(solution)/shard_map/ppermute | solution.py:26
  546.0 25.3 %collective-permute-start.23 = (bf16[2,2,2,48,768]{4,3,2,1,0:T(8,128)(2,1)}, bf16[2,2,2,48,768]{4,3,2,1,0:T(8,128)(2,1)}, u32[]{:S(2)}, u32[]{:S(2)}) collective-permute-start(bf16[2,2,2,48,768]{4,3,2,1,0:T(8,128)(2,1)} %pad_maximum_fusion.35), channel_id=1, source_target_pairs={{0,2},{1,3},{2,0},{3,1},{4,6},{5,7},{6,4},{7,5},{8,10},{9,11},{10,... | collective-permute-start | bytes 1769480 | tf_op jit(solution)/shard_map/ppermute | solution.py:26
  555.8 19.0 %collective-permute-start.20 = (bf16[2,2,2,48,768]{4,3,2,1,0:T(8,128)(2,1)S(1)}, bf16[2,2,2,48,768]{4,3,2,1,0:T(8,128)(2,1)S(1)}, u32[]{:S(2)}, u32[]{:S(2)}) collective-permute-start(bf16[2,2,2,48,768]{4,3,2,1,0:T(8,128)(2,1)S(1)} %fusion.145), channel_id=1, source_target_pairs={{0,1},{1,0},{2,3},{3,2},{4,5},{5,4},{6,7},{7,6},{8,9},{9,8},{10,11... | collective-permute-start | bytes 1769480 | tf_op jit(solution)/shard_map/ppermute | solution.py:26
  560.6 57.7 %collective-permute-start.31 = (bf16[2,2,2,48,1024]{4,3,2,1,0:T(8,128)(2,1)}, bf16[2,2,2,48,1024]{4,3,2,1,0:T(8,128)(2,1)}, u32[]{:S(2)}, u32[]{:S(2)}) collective-permute-start(bf16[2,2,2,48,1024]{4,3,2,1,0:T(8,128)(2,1)} %fusion.129), channel_id=1, source_target_pairs={{0,2},{1,3},{2,0},{3,1},{4,6},{5,7},{6,4},{7,5},{8,10},{9,11},{10,... | collective-permute-start | bytes 2359304 | tf_op jit(solution)/shard_map/ppermute | solution.py:26
  565.7 55.5 %collective-permute-start.28 = (bf16[2,2,2,48,1024]{4,3,2,1,0:T(8,128)(2,1)}, bf16[2,2,2,48,1024]{4,3,2,1,0:T(8,128)(2,1)}, u32[]{:S(2)}, u32[]{:S(2)}) collective-permute-start(bf16[2,2,2,48,1024]{4,3,2,1,0:T(8,128)(2,1)} %fusion.128), channel_id=1, source_target_pairs={{0,1},{1,0},{2,3},{3,2},{4,5},{5,4},{6,7},{7,6},{8,9},{9,8},{10,11... | collective-permute-start | bytes 2359304 | tf_op jit(solution)/shard_map/ppermute | solution.py:26
  569.0 26.3 %collective-permute-start.40 = (bf16[2,2,96,384]{3,2,1,0:T(8,128)(2,1)S(1)}, bf16[2,2,96,384]{3,2,1,0:T(8,128)(2,1)S(1)}, u32[]{:S(2)}, u32[]{:S(2)}) collective-permute-start(bf16[2,2,96,384]{3,2,1,0:T(8,128)(2,1)S(1)} %fusion.166), channel_id=1, source_target_pairs={{0,1},{1,0},{2,3},{3,2},{4,5},{5,4},{6,7},{7,6},{8,9},{9,8},{10,11... | collective-permute-start | bytes 884744 | tf_op jit(solution)/shard_map/ppermute | solution.py:26
  571.4 25.7 %collective-permute-start.37 = (bf16[2,2,96,384]{3,2,1,0:T(8,128)(2,1)S(1)}, bf16[2,2,96,384]{3,2,1,0:T(8,128)(2,1)S(1)}, u32[]{:S(2)}, u32[]{:S(2)}) collective-permute-start(bf16[2,2,96,384]{3,2,1,0:T(8,128)(2,1)S(1)} %fusion.165), channel_id=1, source_target_pairs={{0,2},{1,3},{2,0},{3,1},{4,6},{5,7},{6,4},{7,5},{8,10},{9,11},{10,... | collective-permute-start | bytes 884744 | tf_op jit(solution)/shard_map/ppermute | solution.py:26
  574.7 25.5 %collective-permute-start.24 = (bf16[2,2,48,768]{3,2,1,0:T(8,128)(2,1)S(1)}, bf16[2,2,48,768]{3,2,1,0:T(8,128)(2,1)S(1)}, u32[]{:S(2)}, u32[]{:S(2)}) collective-permute-start(bf16[2,2,48,768]{3,2,1,0:T(8,128)(2,1)S(1)} %pad_maximum_fusion.40), channel_id=1, source_target_pairs={{0,1},{1,0},{2,3},{3,2},{4,5},{5,4},{6,7},{7,6},{8,9},{9,8},{10,11... | collective-permute-start | bytes 884744 | tf_op jit(solution)/shard_map/ppermute | solution.py:26
  595.3 6.7 %collective-permute-start.21 = (bf16[2,2,48,768]{3,2,1,0:T(8,128)(2,1)S(1)}, bf16[2,2,48,768]{3,2,1,0:T(8,128)(2,1)S(1)}, u32[]{:S(2)}, u32[]{:S(2)}) collective-permute-start(bf16[2,2,48,768]{3,2,1,0:T(8,128)(2,1)S(1)} %fusion.164), channel_id=1, source_target_pairs={{0,2},{1,3},{2,0},{3,1},{4,6},{5,7},{6,4},{7,5},{8,10},{9,11},{10,... | collective-permute-start | bytes 884744 | tf_op jit(solution)/shard_map/ppermute | solution.py:26
  597.2 7.4 %collective-permute-start.41 = (bf16[2,96,768]{2,1,0:T(8,128)(2,1)S(1)}, bf16[2,96,768]{2,1,0:T(8,128)(2,1)S(1)}, u32[]{:S(2)}, u32[]{:S(2)}) collective-permute-start(bf16[2,96,768]{2,1,0:T(8,128)(2,1)S(1)} %fusion.169), channel_id=1, source_target_pairs={{0,4},{1,5},{2,6},{3,7},{4,0},{5,1},{6,2},{7,3},{8,12},{9,13},{10,... | collective-permute-start | bytes 884744 | tf_op jit(solution)/shard_map/ppermute | solution.py:26
  603.1 10.5 %copy-start.61 = (f32[2,2,48,768]{3,2,1,0:T(8,128)S(1)}, f32[2,2,48,768]{3,2,1,0:T(8,128)}, u32[]{:S(2)}) copy-start(f32[2,2,48,768]{3,2,1,0:T(8,128)} %copy-done.60) | copy-start | bytes 1769476
  603.1 10.5 %copy-start.63 = (f32[2,2,48,704]{3,2,1,0:T(8,128)S(1)}, f32[2,2,48,704]{3,2,1,0:T(8,128)}, u32[]{:S(2)}) copy-start(f32[2,2,48,704]{3,2,1,0:T(8,128)} %copy-done.62) | copy-start | bytes 1622020
  603.1 10.3 %collective-permute-start.25 = (bf16[2,48,1536]{2,1,0:T(8,128)(2,1)S(1)}, bf16[2,48,1536]{2,1,0:T(8,128)(2,1)S(1)}, u32[]{:S(2)}, u32[]{:S(2)}) collective-permute-start(bf16[2,48,1536]{2,1,0:T(8,128)(2,1)S(1)} %concatenate.165), channel_id=1, source_target_pairs={{0,4},{1,5},{2,6},{3,7},{4,0},{5,1},{6,2},{7,3},{8,12},{9,13},{10,... | collective-permute-start | bytes 884744 | tf_op jit(solution)/shard_map/ppermute | solution.py:26
  605.4 29.0 %collective-permute-start.42 = (bf16[96,768]{1,0:T(8,128)(2,1)}, bf16[96,768]{1,0:T(8,128)(2,1)}, u32[]{:S(2)}, u32[]{:S(2)}) collective-permute-start(bf16[96,768]{1,0:T(8,128)(2,1)} %fusion.174), channel_id=1, source_target_pairs={{0,8},{1,9},{2,10},{3,11},{4,12},{5,13},{6,14},{7,15},{8,0},{9,1},... | collective-permute-start | bytes 442376 | tf_op jit(solution)/shard_map/ppermute | solution.py:26
  614.6 10.0 %collective-permute-start.26 = (bf16[48,1536]{1,0:T(8,128)(2,1)S(1)}, bf16[48,1536]{1,0:T(8,128)(2,1)S(1)}, u32[]{:S(2)}, u32[]{:S(2)}) collective-permute-start(bf16[48,1536]{1,0:T(8,128)(2,1)S(1)} %concatenate.167), channel_id=1, source_target_pairs={{0,8},{1,9},{2,10},{3,11},{4,12},{5,13},{6,14},{7,15},{8,0},{9,1},... | collective-permute-start | bytes 442376 | tf_op jit(solution)/shard_map/ppermute | solution.py:26
  620.7 14.8 %collective-permute-start.32 = (bf16[2,2,48,1024]{3,2,1,0:T(8,128)(2,1)}, bf16[2,2,48,1024]{3,2,1,0:T(8,128)(2,1)}, u32[]{:S(2)}, u32[]{:S(2)}) collective-permute-start(bf16[2,2,48,1024]{3,2,1,0:T(8,128)(2,1)} %fusion.159), channel_id=1, source_target_pairs={{0,1},{1,0},{2,3},{3,2},{4,5},{5,4},{6,7},{7,6},{8,9},{9,8},{10,11... | collective-permute-start | bytes 1179656 | tf_op jit(solution)/shard_map/ppermute | solution.py:26
  623.4 13.3 %collective-permute-start.29 = (bf16[2,2,48,1024]{3,2,1,0:T(8,128)(2,1)}, bf16[2,2,48,1024]{3,2,1,0:T(8,128)(2,1)}, u32[]{:S(2)}, u32[]{:S(2)}) collective-permute-start(bf16[2,2,48,1024]{3,2,1,0:T(8,128)(2,1)} %fusion.158), channel_id=1, source_target_pairs={{0,2},{1,3},{2,0},{3,1},{4,6},{5,7},{6,4},{7,5},{8,10},{9,11},{10,... | collective-permute-start | bytes 1179656 | tf_op jit(solution)/shard_map/ppermute | solution.py:26
  634.4 14.4 %copy-start.139 = (f32[96]{0:T(128)}, f32[96]{0:T(128)S(1)}, u32[]{:S(2)}) copy-start(f32[96]{0:T(128)S(1)} %reshape.432) | copy-start | bytes 1156
  638.0 8.5 %collective-permute-start.33 = (bf16[2,48,2048]{2,1,0:T(8,128)(2,1)S(1)}, bf16[2,48,2048]{2,1,0:T(8,128)(2,1)S(1)}, u32[]{:S(2)}, u32[]{:S(2)}) collective-permute-start(bf16[2,48,2048]{2,1,0:T(8,128)(2,1)S(1)} %fusion.162), channel_id=1, source_target_pairs={{0,4},{1,5},{2,6},{3,7},{4,0},{5,1},{6,2},{7,3},{8,12},{9,13},{10,... | collective-permute-start | bytes 1179656 | tf_op jit(solution)/shard_map/ppermute | solution.py:26
  641.0 14.5 %copy-start.99 = (f32[48,1536]{1,0:T(8,128)S(1)}, f32[48,1536]{1,0:T(8,128)}, u32[]{:S(2)}) copy-start(f32[48,1536]{1,0:T(8,128)} %param.37) | copy-start | bytes 884740
  641.0 14.5 %copy-start.109 = (f32[48,1536]{1,0:T(8,128)S(1)}, f32[48,1536]{1,0:T(8,128)}, u32[]{:S(2)}) copy-start(f32[48,1536]{1,0:T(8,128)} %param.39) | copy-start | bytes 884740
  641.0 14.5 %copy-start.110 = (f32[48,1536]{1,0:T(8,128)S(1)}, f32[48,1536]{1,0:T(8,128)}, u32[]{:S(2)}) copy-start(f32[48,1536]{1,0:T(8,128)} %param.38) | copy-start | bytes 884740
  646.7 8.7 %collective-permute-start.34 = (bf16[48,2048]{1,0:T(8,128)(2,1)S(1)}, bf16[48,2048]{1,0:T(8,128)(2,1)S(1)}, u32[]{:S(2)}, u32[]{:S(2)}) collective-permute-start(bf16[48,2048]{1,0:T(8,128)(2,1)S(1)} %fusion.173), channel_id=1, source_target_pairs={{0,8},{1,9},{2,10},{3,11},{4,12},{5,13},{6,14},{7,15},{8,0},{9,1},... | collective-permute-start | bytes 589832 | tf_op jit(solution)/shard_map/ppermute | solution.py:26
  (135 other events, 557.2 us)
Sparse Core Ops, SparseCore 0:
  17.7 77.5 all-gather.1
